TPU v7x, 32 devices: a whole 2x2x4 slice. The times are simulated.
32 devices in a mesh: beam: 2 (over y), freq: 8 (over z, x), tm: 2 (over core).
Axes of the slice: x: 2, y: 2, z: 4, core: 2. Of those that a mesh axis runs over, the one named last changes fastest.
Arguments:
- voltages: bfloat16 [4, 8192, 1024], P('beam', 'tm', 'freq'), parts along dimension 0, may hold values from -6 to 6
- pfb_taps: float32 [16, 128], replicated, may hold values from -1.5 to 1.5
- local_shift: int32 [7, 512], P(None, 'freq'), may hold values from 0 to 7
- cross_shift: int32 [3, 64], P(None, 'freq'), may hold values from 0 to 31, as said below
- tap_index: int32 [32, 128], replicated, may hold values from 0 to 255
- tap_weight: float32 [32, 128], replicated, may hold values from -0.5 to 0.5
Outputs:
- dedispersed: float32 [128, 8192], P(('beam', 'freq'), 'tm'), parts along dimension 0
- scores: float32 [128, 32, 256], P(('beam', 'freq'), None, 'tm'), parts along dimension 0
There are 2 independent parts, one for each index of `beam`. A program takes and returns all parts, laid end to end along the dimension named above; an argument that names none is the same for every part. Nothing has to cross between parts.
Inputs may be any that keep to these rules, and one draw needn't show every extreme that they name: `cross_shift`: row j holds values 0 to 8 * 2**j - 1, and reaches that value.
All inputs are finite; a program needn't handle non-finite values.
Results may differ from a plain program's by a relative error of at most 0.0003.
Values may be sent and summed in bfloat16 or wider, within the bound.
No kernel may reach another device: no remote copies, remote signals or barrier semaphores. Data moves between devices by JAX's collectives and lax.ppermute only.
A program may use at most 64 MiB of HBM per device.

v0:
```python
import math

import jax
import jax.numpy as jnp
import numpy as np
from jax import lax
from jax.experimental import pallas as pl
from jax.experimental.pallas import tpu as pltpu
from jax.sharding import PartitionSpec as P

LSHIFT = 8
STRIDE = 32
WIN = 256
SET = 5
LARGEST = 32000.0
LANES = 128
ROWS = 8
BF = jnp.bfloat16
F32 = jnp.float32
NT = (((1,), (1,)), ((), ()))
VMEM = pl.BlockSpec(memory_space=pltpu.VMEM)
SMEM = pl.BlockSpec(memory_space=pltpu.SMEM)
ANY = pl.BlockSpec(memory_space=pl.ANY)
PARAMS = pltpu.CompilerParams(vmem_limit_bytes=48 * 1024 * 1024)


def round_up(value, multiple):
    return -(-value // multiple) * multiple


def whole(array):
    return pl.BlockSpec(array.shape, lambda *_: (0,) * array.ndim)


def tile(k):
    return slice(k * LANES, (k + 1) * LANES)


def split(x):
    high = x.astype(BF)
    return high, (x - high.astype(F32)).astype(BF)


def lanes():
    return lax.broadcasted_iota(jnp.int32, (ROWS, LANES), 1)


def rotated(x, index):
    return jnp.take_along_axis(x, index, axis=1, mode="promise_in_bounds")


def merged(leading, trailing, shifts, lead_tiles):
    lane = lanes()
    index = (lane - shifts) & (LANES - 1)
    inside = lane >= shifts
    out = []
    for k, (lead, trail) in enumerate(zip(leading, trailing)):
        if k in (0, lead_tiles):
            before = jnp.zeros((ROWS, LANES), F32)
        turned = rotated(trail, index)
        out.append(lead + jnp.where(inside, turned, before))
        before = turned
    return out


def dft_table(channels, group):
    place = np.arange(channels)
    number = (place % (channels // group)) * group + place // (channels // group)
    phase = (np.arange(channels)[:, None] * number[None, :]) % channels
    angle = phase * (2.0 * np.pi / channels)
    cosine, sine = np.cos(angle), np.sin(angle)
    return np.block([[cosine, -sine], [sine, cosine]]).astype(np.float32)


def spread_table(tiles, blocks):
    trials = LANES // tiles
    table = np.zeros((blocks, trials, tiles, trials, tiles * blocks), np.float32)
    for block in range(blocks):
        for trial in range(trials):
            for number in range(tiles):
                table[block, trial, number, trial, number * blocks + block] = 1.0
    return table.reshape(blocks * LANES, -1).astype(jnp.bfloat16)


def front_kernel(
    sizes, info, volts, beside, packed, out, words, notes, held, samples, *scratch
):
    filtered, spectra = (scratch[:2], scratch[2:4]), scratch[4:6]
    series, sums, arrived = scratch[6:]
    frames, lead, tail, chunk_tiles, pieces, tap_count, level_count, columns = sizes
    channels = volts.shape[2]
    taps_at, shifts_at = 2 * channels, 2 * channels + tap_count
    group_count = channels // ROWS
    margin = round_up(tap_count, 16)
    halo_rows = beside.shape[1]
    first, last = info[0] == 0, info[1] == 1
    piece = frames // pieces

    def copies(number):
        rows = slice(number * piece, (number + 1) * piece)
        return pltpu.make_async_copy(volts.at[:, rows, :], held.at[:, rows, :], arrived.at[number])

    copies(0).start()
    for number in range(1, pieces):
        copies(number).start()

    place = lax.broadcasted_iota(jnp.int32, (channels, columns), 0)
    column = lax.broadcasted_iota(jnp.int32, (channels, columns), 1)
    channel = (place & (ROWS - 1)) * group_count + (place >> (ROWS.bit_length() - 1))
    single_levels = group_count.bit_length() - 1

    def picked(hit, level):
        row = jnp.broadcast_to(packed[shifts_at + level : shifts_at + level + 1, :columns], (LANES, columns))
        return lax.dot_general(hit.astype(F32), row, NT, preferred_element_type=F32)

    total = jnp.zeros((channels, LANES), F32)
    for level in range(single_levels):
        trailing = (channel >> level & 1) == 1
        spot = (channel >> (level + 1)) << level
        total = total + picked(jnp.logical_and(trailing, column == spot), level)
    total = total.astype(jnp.int32)
    shift = [total[j * ROWS : (j + 1) * ROWS] for j in range(group_count)]
    lane = lanes()
    lead_tiles, main_tiles, tail_tiles = lead // LANES, frames // LANES, tail // LANES
    tile_count = lead_tiles + main_tiles + tail_tiles

    def convert(number):
        if number == pieces:
            for part in range(2):
                before = beside[part, halo_rows - lead - margin :, :].astype(F32)
                samples[part, : lead + margin, :] = jnp.where(first, 0.0, before)
                after = beside[part, :tail, :].astype(F32)
                samples[part, lead + margin + frames :, :] = jnp.where(last, 0.0, after)
            return
        copies(number).wait()
        rows = slice(number * piece, (number + 1) * piece)
        at = lead + margin + number * piece
        for part in range(2):
            samples[part, at : at + piece, :] = held[part, rows, :].astype(F32)

    def filter_tile(number, into):
        for part in range(2):
            base = number * LANES + margin
            value = samples[part, base : base + LANES, :] * packed[taps_at : taps_at + 1, :channels]
            for k in range(1, tap_count):
                value = value + samples[part, base - k : base - k + LANES, :] * packed[taps_at + k : taps_at + k + 1, :channels]
            filtered[into[0]][part][into[1] * LANES : (into[1] + 1) * LANES, :] = value

    def transform(slot, count):
        rows = slice(0, count * LANES)
        both = jnp.concatenate([filtered[slot][0][rows, :], filtered[slot][1][rows, :]], axis=1)
        spectra[slot][rows, :] = jnp.dot(
            both, packed[:taps_at, :], preferred_element_type=F32, precision=lax.Precision.HIGH
        )

    def collapse_tile(number, slot, sub, earlier):
        real, imag = spectra[slot][tile(sub), :channels], spectra[slot][tile(sub), channels:]
        power = (real * real + imag * imag).T
        counted = lead_tiles <= number < lead_tiles + main_tiles
        acc = jnp.zeros((ROWS, LANES), F32)
        now = []
        for j in range(group_count):
            rows = slice(j * ROWS, (j + 1) * ROWS)
            value = power[rows]
            turned = rotated(value, (lane - shift[j]) & (LANES - 1))
            acc = acc + jnp.where(lane >= shift[j], turned, earlier[j])
            now.append(turned)
            if counted:
                sums[rows] += value
        series[:, tile(lead_tiles + number)] = acc
        return now

    sums[...] = jnp.zeros_like(sums)
    starts = list(range(0, tile_count, chunk_tiles)) + [tile_count]
    chunks = len(starts) - 1
    earlier = [jnp.zeros((ROWS, LANES), F32)] * group_count
    converted = 0
    convert(pieces)
    for step in range(chunks + 2):
        if step < chunks:
            needed = min(pieces, -(-((starts[step + 1] - lead_tiles) * LANES) // piece))
            while converted < needed:
                convert(converted)
                converted += 1
        if 1 <= step <= chunks:
            transform((step - 1) % 2, starts[step] - starts[step - 1])
        for sub in range(chunk_tiles):
            if step < chunks and starts[step] + sub < starts[step + 1]:
                filter_tile(starts[step] + sub, (step % 2, sub))
            if step >= 2 and starts[step - 2] + sub < starts[step - 1]:
                earlier = collapse_tile(starts[step - 2] + sub, step % 2, sub, earlier)

    settled = jnp.zeros((ROWS, LANES), F32)
    begun = jnp.zeros((ROWS, LANES), F32)
    for j in range(group_count):
        rows = slice(j * ROWS, (j + 1) * ROWS)
        channel_sum = jnp.broadcast_to(jnp.sum(sums[rows], axis=1, keepdims=True), (ROWS, LANES))
        settled = settled + channel_sum
        begun = begun + jnp.where(lane >= shift[j], channel_sum, 0.0)
    series[:, :LANES] = begun
    for k in range(1, lead_tiles):
        series[:, tile(k)] = settled

    tiles = [series[:, tile(k)] for k in range(lead_tiles + tile_count)]
    row = lax.broadcasted_iota(jnp.int32, (ROWS, LANES), 0)
    slot_row = lax.broadcasted_iota(jnp.int32, (ROWS, columns), 0)
    slot_column = lax.broadcasted_iota(jnp.int32, (ROWS, columns), 1)
    for step in range(level_count - single_levels):
        level = single_levels + step
        distance = 2**step
        upper = (row & distance) > 0
        leading = [jnp.where(upper, pltpu.roll(x, distance, 0), x) for x in tiles]
        trailing = [jnp.where(upper, x, pltpu.roll(x, ROWS - distance, 0)) for x in tiles]
        spot = ((slot_row >> (step + 1)) << level) + (slot_row & (2 * distance - 1))
        tiles = merged(leading, trailing, picked(slot_column == spot, level).astype(jnp.int32), lead_tiles)
    for k, x in enumerate(tiles):
        out[:, tile(k)] = x
    encode(tiles, lead_tiles, words, notes)


def pieces_of(count, lead_tiles):
    starts = [0] + list(range(lead_tiles, count, SET)) + [count]
    return [range(at, to) for at, to in zip(starts[:-1], starts[1:])]


def encode(tiles, lead_tiles, words, notes):
    lane = lanes()
    body = tiles[lead_tiles:]
    for k in range(lead_tiles):
        notes[:, tile(k)] = tiles[k]
    note = jnp.zeros((ROWS, LANES), F32)
    steps = []
    for number, members in enumerate(pieces_of(len(body), lead_tiles)):
        top, bottom = body[members[0]], body[members[0]]
        for k in members[1:]:
            top, bottom = jnp.maximum(top, body[k]), jnp.minimum(bottom, body[k])
        top = jnp.max(top, axis=1, keepdims=True)
        bottom = jnp.min(bottom, axis=1, keepdims=True)
        middle = 0.5 * top + 0.5 * bottom
        half = jnp.maximum(0.5 * top - 0.5 * bottom, 1e-30)
        note = jnp.where(lane == 2 * number, middle, note)
        note = jnp.where(lane == 2 * number + 1, half * (1.0 / LARGEST), note)
        per_step = jnp.broadcast_to(LARGEST / half, (ROWS, LANES))
        middle = jnp.broadcast_to(middle, (ROWS, LANES))
        steps.extend(jnp.floor((body[k] - middle) * per_step + 0.5) for k in members)
    notes[:, tile(lead_tiles)] = note
    if len(steps) % 2:
        steps.append(jnp.zeros((ROWS, LANES), F32))
    for k in range(len(steps) // 2):
        pair = jnp.concatenate([steps[2 * k], steps[2 * k + 1]], axis=0)
        words[:, tile(k)] = pair.astype(jnp.int32).astype(jnp.int16)


def decode(words, notes, count, lead_tiles):
    tiles = [notes[:, tile(k)] for k in range(lead_tiles)]
    note = notes[:, tile(lead_tiles)]
    steps = []
    for k in range(words.shape[1] // LANES):
        pair = words[:, tile(k)].astype(jnp.int32).astype(F32)
        steps += [pair[:ROWS], pair[ROWS:]]
    for number, members in enumerate(pieces_of(count - lead_tiles, lead_tiles)):
        middle = jnp.broadcast_to(note[:, 2 * number : 2 * number + 1], (ROWS, LANES))
        size = jnp.broadcast_to(note[:, 2 * number + 1 : 2 * number + 2], (ROWS, LANES))
        tiles.extend(steps[k] * size + middle for k in members)
    return tiles


def ordered(mine, theirs, is_upper):
    leading = [jnp.where(is_upper, y, x) for x, y in zip(mine, theirs)]
    trailing = [jnp.where(is_upper, x, y) for x, y in zip(mine, theirs)]
    return leading, trailing


def tiles_of(ref):
    return [ref[:, tile(k)] for k in range(ref.shape[1] // LANES)]


def merge_kernel(level, lead_tiles, info, own, words, notes, other, across, shifts, out, *sent):
    mine = tiles_of(own)
    theirs = decode(words, notes, len(mine), lead_tiles)
    if level == 0:
        for k in range(lead_tiles):
            mine[k], theirs[k] = mine[k] + other[:, tile(k)], theirs[k] + across[:, tile(k)]
    tiles = merged(*ordered(mine, theirs, info[2 + level] == 1), shifts[level], lead_tiles)
    for k, x in enumerate(tiles):
        out[:, tile(k)] = x
    if sent:
        encode(tiles, lead_tiles, *sent)


def back_kernel(level, sizes, info, own, words, notes, shifts, weights, spread, dedispersed, scores, steps):
    frames, lead, tail, factor, window_count, stations = sizes
    first, last = info[0] == 0, info[1] == 1
    lead_tiles, main_tiles, tail_tiles = lead // LANES, frames // LANES, tail // LANES
    if level is None:
        series = tiles_of(own)
    else:
        is_upper = info[2 + level] == 1
        mine = tiles_of(own)
        theirs = decode(words, notes, len(mine), lead_tiles)
        series = merged(*ordered(mine, theirs, is_upper), shifts[level], lead_tiles)
    means = [series[k] * (1.0 / window_count) for k in range(lead_tiles)]
    settled = jnp.broadcast_to(means[-1][:, LANES - 1 :], (ROWS, LANES))
    for k in range(main_tiles + tail_tiles):
        mean = jnp.where(first, means[k], settled) if k < lead_tiles else settled
        value = (series[2 * lead_tiles + k] - mean) * factor
        if k < main_tiles:
            dedispersed[:, tile(k)] = value
        else:
            value = jnp.where(last, 0.0, value)
        steps[k * ROWS : (k + 1) * ROWS, :] = value

    reach = tail_tiles + 1
    parts = []
    for q in range(reach):
        parts.append(
            jnp.concatenate([steps[pl.ds(d + ROWS * q, main_tiles, stride=ROWS), :] for d in range(ROWS)], axis=0)
        )
    operand = jnp.concatenate(parts, axis=1)
    high, low = split(operand)
    weight_high, weight_low = split(weights[...])
    product = lax.dot_general(
        jnp.concatenate([weight_high, weight_high, weight_low], axis=1),
        jnp.concatenate([high, low, high], axis=1),
        NT,
        preferred_element_type=F32,
    )
    blocks = LANES // STRIDE
    templates = product.shape[0] // blocks
    sets = product.shape[1] // LANES
    grouped = jnp.concatenate(
        [
            jnp.concatenate([product[i * templates : (i + 1) * templates, tile(a)] for i in range(blocks)], axis=1)
            for a in range(sets)
        ],
        axis=0,
    )
    one = grouped.astype(BF)
    rest = grouped - one.astype(F32)
    two = rest.astype(BF)
    three = (rest - two.astype(F32)).astype(BF)
    placed = jnp.dot(jnp.concatenate([one, two, three], axis=0), spread[...], preferred_element_type=F32)
    count = sets * templates
    placed = placed[:count] + placed[count : 2 * count] + placed[2 * count :]
    trials = LANES // main_tiles
    positions = main_tiles * blocks
    for a in range(sets):
        for d in range(trials):
            scores[a * trials + d] = placed[a * templates : (a + 1) * templates, d * positions : (d + 1) * positions]


def swapped(x, axis, distance):
    return lax.ppermute(x, axis, [(i, i ^ distance) for i in range(lax.axis_size(axis))])


def template_weights(tap_index, tap_weight, reach):
    hit = tap_index[:, :, None] == jnp.arange(WIN, dtype=jnp.int32)[None, None, :]
    template = jnp.sum(jnp.where(hit, tap_weight[:, :, None], 0.0), axis=1)
    width = reach * LANES
    rows = [
        jnp.pad(template, ((0, 0), (i * STRIDE, width - WIN - i * STRIDE))) for i in range(LANES // STRIDE)
    ]
    return jnp.concatenate(rows, axis=0)


def wide_merge(own, partner, is_upper, shifts):
    leading = jnp.where(is_upper, partner, own)
    trailing = jnp.where(is_upper, own, partner)
    place = jnp.arange(own.shape[1], dtype=jnp.int32)[None, :] - shifts[:, None]
    picked = jnp.take_along_axis(trailing, jnp.maximum(place, 0), axis=1)
    return leading + jnp.where(place >= 0, picked, 0.0)


def on_device(voltages, pfb_taps, local_shift, cross_shift, tap_index, tap_weight):
    frames, channels = voltages.shape[1:]
    tap_count = pfb_taps.shape[0]
    trials = cross_shift.shape[1]
    local_levels = local_shift.shape[0]
    tm_size, freq_size = lax.axis_size("tm"), lax.axis_size("freq")
    levels = freq_size.bit_length() - 1
    group = channels // trials
    margin = round_up(tap_count, 16)
    cross_reach = sum(trials * 2**level - 1 for level in range(levels))
    lead = round_up(local_levels * (LSHIFT - 1) + cross_reach, LANES)
    tail = round_up(WIN - STRIDE, LANES)

    time, freq = lax.axis_index("tm"), lax.axis_index("freq")
    info = jnp.stack(
        [time, (time == tm_size - 1).astype(jnp.int32)] + [freq >> level & 1 for level in range(max(levels, 1))]
    ).astype(jnp.int32)
    halo_rows = round_up(max(lead + margin, tail), 16)
    if tm_size == 2:
        start = jnp.where(time == 0, frames - halo_rows, 0)
        sent = lax.dynamic_slice_in_dim(voltages, start, halo_rows, axis=1)
        halo = swapped(sent, "tm", 1)
    else:
        raise NotImplementedError("tm")

    chunk_tiles, pieces = 5, 8
    table = jnp.asarray(dft_table(channels, group))
    extended = lead + frames + tail
    width = lead + extended

    sizes = (frames, lead, tail, chunk_tiles, pieces, tap_count) + local_shift.shape
    wide = 2 * channels
    spare = ((0, -(tap_count + local_levels) % ROWS), (0, wide - local_shift.shape[1]))
    packed = jnp.concatenate(
        [table, jnp.pad(pfb_taps, ((0, 0), (0, wide - channels))), jnp.pad(local_shift.astype(F32), spare)], axis=0
    )

    def front(*refs):
        front_kernel(sizes, *refs)

    lead_tiles, body_tiles = lead // LANES, extended // LANES
    sent_shapes = (
        jax.ShapeDtypeStruct((2 * ROWS, -(-body_tiles // 2) * LANES), jnp.int16),
        jax.ShapeDtypeStruct((trials, lead + LANES), F32),
    )
    series_shape = jax.ShapeDtypeStruct((trials, width), F32)
    series, *sent = pl.pallas_call(
        front,
        out_shape=(series_shape,) + sent_shapes,
        in_specs=[SMEM, ANY, VMEM, VMEM],
        out_specs=(VMEM,) * 3,
        scratch_shapes=[
            pltpu.VMEM(voltages.shape, BF),
            pltpu.VMEM((2, margin + extended, channels), F32),
            *[pltpu.VMEM((chunk_tiles * LANES, channels), F32)] * 4,
            *[pltpu.VMEM((chunk_tiles * LANES, 2 * channels), F32)] * 2,
            pltpu.VMEM((trials, width), F32),
            pltpu.VMEM((channels, LANES), F32),
            pltpu.SemaphoreType.DMA((pieces,)),
        ],
        compiler_params=pltpu.CompilerParams(vmem_limit_bytes=52 * 1024 * 1024),
        cost_estimate=pl.CostEstimate(flops=2 * 10**10, bytes_accessed=4096, transcendentals=0),
        name="front",
    )(info, voltages, halo, packed)

    shift_rows = jnp.broadcast_to(cross_shift[:, :, None], cross_shift.shape + (LANES,))
    (tap_index, tap_weight), sent = lax.optimization_barrier(((tap_index, tap_weight), sent))
    weights = template_weights(tap_index, tap_weight, tail // LANES + 1)
    short = [level for level in range(levels) if trials * 2**level <= LANES]
    fused = len(short) == levels > 1
    other = swapped(sent[1][:, :lead], "tm", 1)
    for level in range(levels - 1 if fused else levels):
        if level in short:
            received = [swapped(x, "freq", 2**level) for x in sent]
            if level == 0:
                across = swapped(other, "freq", 1)
                received[0], weights = lax.optimization_barrier((received[0], weights))
            shapes = (series_shape,) + (sent_shapes if level + 1 in short else ())

            def merge(*refs, level=level):
                merge_kernel(level, lead_tiles, *refs)

            series, *sent = pl.pallas_call(
                merge,
                out_shape=shapes,
                in_specs=[SMEM] + [VMEM] * 6,
                out_specs=(VMEM,) * len(shapes),
                compiler_params=PARAMS,
                name="merge",
            )(info, series, *received, other, across, shift_rows)
        else:
            partner = swapped(series, "freq", 2**level)
            series = wide_merge(series, partner, info[2 + level] == 1, cross_shift[level])

    if fused:
        last_level = levels - 1
        received = [swapped(x, "freq", 2**last_level) for x in sent]
    else:
        last_level = None
        received = [other, other]

    templates = tap_index.shape[0]
    spread = jnp.asarray(spread_table(frames // LANES, LANES // STRIDE))
    factor = 1.0 / (channels * math.sqrt(channels * freq_size))

    def back(*refs):
        back_kernel(last_level, (frames, lead, tail, factor, frames * tm_size, STRIDE), *refs)

    return pl.pallas_call(
        back,
        out_shape=(
            jax.ShapeDtypeStruct((trials, frames), F32),
            jax.ShapeDtypeStruct((trials, templates, frames // STRIDE), F32),
        ),
        in_specs=[SMEM] + [VMEM] * 6,
        out_specs=(VMEM, VMEM),
        scratch_shapes=[pltpu.VMEM(((frames + tail) // LANES * ROWS, LANES), F32)],
        compiler_params=PARAMS,
        name="back",
    )(info, series, *received, shift_rows, weights, spread)


def solution(mesh):
    return jax.shard_map(
        on_device,
        mesh=mesh,
        in_specs=(P("beam", "tm", "freq"), P(), P(None, "freq"), P(None, "freq"), P(), P()),
        out_specs=(P(("beam", "freq"), "tm"), P(("beam", "freq"), None, "tm")),
        check_vma=False,
    )
```

profile of v0, /device:TPU:0, one launch (start us, length us, event | category | flops | bytes accessed | tf_op | source)
XLA Modules:
  0.0 40.1 jit_solution(3202276846046727071)
XLA Ops:
  0.6 0.9 %constant_dynamic-slice_fusion = bf16[2,256,128]{2,1,0:T(8,128)(2,1)S(1)} fusion(bf16[2,4096,128]{2,1,0:T(8,128)(2,1)} %refs_1_.1, s32[]{:T(128)S(6)} %select_n.9), kind=kLoop, calls=%fused_computation.19 | loop fusion | bytes 262148 | tf_op jit(solution)/shard_map/dynamic_slice | solution.py:394
  1.6 0.5 %collective-permute-start = (bf16[2,256,128]{2,1,0:T(8,128)(2,1)S(1)}, bf16[2,256,128]{2,1,0:T(8,128)(2,1)S(1)}, u32[]{:S(2)}, u32[]{:S(2)}) collective-permute-start(bf16[2,256,128]{2,1,0:T(8,128)(2,1)S(1)} %constant_dynamic-slice_fusion), channel_id=1, source_target_pairs={{0,1},{1,0},{2,3},{3,2},{4,5},{5,4},{6,7},{7,6},{8,9},{9,8},{10,11... | collective-permute-start | bytes 393224 | tf_op jit(solution)/shard_map/ppermute | solution.py:353
  2.1 0.7 %convert_element_type.16 = f32[7,64]{1,0:T(8,128)S(1)} convert(s32[7,64]{1,0:T(8,128)} %param.10) | non-fusion elementwise | flops 448 | bytes 3584 | tf_op jit(solution)/shard_map/convert_element_type | solution.py:408
  2.8 0.1 stack.27.refs_0_
  2.9 1.0 %select_maximum_fusion.refs_3_ = f32[280,256]{1,0:T(8,128)S(1)} fusion(f32[7,64]{1,0:T(8,128)S(1)} %convert_element_type.16, f32[16,128]{1,0:T(8,128)} %param.9, f32[256,256]{1,0:T(8,128)} %constant.25.clone), kind=kLoop, calls=%fused_computation.8 | loop fusion | flops 573440 | bytes 558848 | tf_op jit(solution)/shard_map/concatenate | solution.py:407
  3.8 0.0 copy-start.1
  3.9 0.0 copy-start.2
  3.9 0.0 copy-start.3
  3.9 0.0 copy-start
  3.9 0.0 collective-permute-done.refs_2_
  3.9 11.4 %front.1 = (f32[8,4608]{1,0:T(8,128)S(1)}, s16[16,2304]{1,0:T(8,128)(2,1)S(1)}, f32[8,256]{1,0:T(8,128)S(1)}) custom-call(s32[5]{0:T(128)S(1)} %stack.27.refs_0_, bf16[2,4096,128]{2,1,0:T(8,128)(2,1)} %refs_1_.1, bf16[2,256,128]{2,1,0:T(8,128)(2,1)S(1)} %collective-permute-done.refs_2_, f32[280,256]{1,0:T(8,128)S(1)} %select_maximum_fusion.refs_3_), custom_call_target="tpu_custom_call" | custom-call | flops 20000000000 | bytes 4096 | tf_op jit(solution)/shard_map/front/pallas_call | solution.py:420
  15.3 2.6 %collective-permute-start.2 = (f32[8,256]{1,0:T(8,128)S(1)}, f32[8,256]{1,0:T(8,128)S(1)}, u32[]{:S(2)}, u32[]{:S(2)}) collective-permute-start(f32[8,256]{1,0:T(8,128)S(1)} %get-tuple-element.24), channel_id=1, source_target_pairs={{0,2},{2,0},{4,6},{6,4},{8,10},{10,8},{12,14},{14,12},{1,3},{3,1},... | collective-permute-start | bytes 24584 | tf_op jit(solution)/shard_map/ppermute | solution.py:353
  17.9 0.2 collective-permute-start.3
  18.1 0.4 collective-permute-start.1
  18.5 1.4 %select_reduce_fusion = f32[32,256]{1,0:T(8,128)S(1)} fusion(f32[32,128]{1,0:T(8,128)S(1)} %copy-done.1, s32[32,128]{1,0:T(8,128)S(1)} %copy-done.2), kind=kLoop, calls=%fused_computation | loop fusion | flops 3137536 | bytes 65536 | tf_op jit(solution)/shard_map/reduce_sum | solution.py:358
  19.9 1.7 %collective-permute-start.4 = (f32[8,128]{1,0:T(8,128)S(1)}, f32[8,128]{1,0:T(8,128)S(1)}, u32[]{:S(2)}, u32[]{:S(2)}) collective-permute-start(f32[8,128]{1,0:T(8,128)S(1)} %collective-permute-done.3.refs_4_), channel_id=1, source_target_pairs={{0,2},{2,0},{4,6},{6,4},{8,10},{10,8},{12,14},{14,12},{1,3},{3,1},... | collective-permute-start | bytes 12296 | tf_op jit(solution)/shard_map/ppermute | solution.py:353
  21.6 0.1 select_maximum_fusion.2.refs_5_
  21.7 0.9 %collective-permute-done.1.refs_2_ = s16[16,2304]{1,0:T(8,128)(2,1)S(1)} collective-permute-done((s16[16,2304]{1,0:T(8,128)(2,1)S(1)}, s16[16,2304]{1,0:T(8,128)(2,1)S(1)}, u32[]{:S(2)}, u32[]{:S(2)}) %collective-permute-start.1) | collective-permute-done | bytes 73760 | tf_op jit(solution)/shard_map/ppermute | solution.py:353
  22.6 0.9 %collective-permute-done.4.refs_5_ = f32[8,128]{1,0:T(8,128)S(1)} collective-permute-done((f32[8,128]{1,0:T(8,128)S(1)}, f32[8,128]{1,0:T(8,128)S(1)}, u32[]{:S(2)}, u32[]{:S(2)}) %collective-permute-start.4) | collective-permute-done | bytes 4128 | tf_op jit(solution)/shard_map/ppermute | solution.py:353
  23.6 0.0 collective-permute-done.2.refs_3_
  23.6 0.1 broadcast_in_dim.23.refs_6_.refs_4_
  23.6 0.8 %merge.2 = (f32[8,4608]{1,0:T(8,128)S(1)}, s16[16,2304]{1,0:T(8,128)(2,1)S(1)}, f32[8,256]{1,0:T(8,128)S(1)}) custom-call(s32[5]{0:T(128)S(1)} %stack.27.refs_0_, f32[8,4608]{1,0:T(8,128)S(1)} %get-tuple-element.17.refs_1_, s16[16,2304]{1,0:T(8,128)(2,1)S(1)} %collective-permute-done.1.refs_2_, f32[8,256]{1,0:T(8,128)S(1)} %collective-permute-done.2.refs_3_, ...), custom_call_target="tpu_custom_call" | custom-call | tf_op jit(solution)/shard_map/merge/pallas_call | solution.py:456
  24.5 1.8 %collective-permute-start.5 = (s16[16,2304]{1,0:T(8,128)(2,1)S(1)}, s16[16,2304]{1,0:T(8,128)(2,1)S(1)}, u32[]{:S(2)}, u32[]{:S(2)}) collective-permute-start(s16[16,2304]{1,0:T(8,128)(2,1)S(1)} %get-tuple-element.26), channel_id=1, source_target_pairs={{0,4},{2,6},{4,0},{6,2},{8,12},{10,14},{12,8},{14,10},{1,5},{3,7},... | collective-permute-start | bytes 221192 | tf_op jit(solution)/shard_map/ppermute | solution.py:353
  26.3 0.3 collective-permute-start.6
  26.6 3.4 %collective-permute-done.6.refs_3_ = f32[8,256]{1,0:T(8,128)S(1)} collective-permute-done((f32[8,256]{1,0:T(8,128)S(1)}, f32[8,256]{1,0:T(8,128)S(1)}, u32[]{:S(2)}, u32[]{:S(2)}) %collective-permute-start.6) | collective-permute-done | bytes 8224 | tf_op jit(solution)/shard_map/ppermute | solution.py:353
  30.0 0.0 collective-permute-done.5.refs_2_
  30.0 0.8 %merge.3 = (f32[8,4608]{1,0:T(8,128)S(1)}, s16[16,2304]{1,0:T(8,128)(2,1)S(1)}, f32[8,256]{1,0:T(8,128)S(1)}) custom-call(s32[5]{0:T(128)S(1)} %stack.27.refs_0_, f32[8,4608]{1,0:T(8,128)S(1)} %get-tuple-element.25.refs_1_, s16[16,2304]{1,0:T(8,128)(2,1)S(1)} %collective-permute-done.5.refs_2_, f32[8,256]{1,0:T(8,128)S(1)} %collective-permute-done.6.refs_3_, ...), custom_call_target="tpu_custom_call" | custom-call | tf_op jit(solution)/shard_map/merge/pallas_call | solution.py:456
  30.8 2.7 %collective-permute-start.7 = (s16[16,2304]{1,0:T(8,128)(2,1)S(1)}, s16[16,2304]{1,0:T(8,128)(2,1)S(1)}, u32[]{:S(2)}, u32[]{:S(2)}) collective-permute-start(s16[16,2304]{1,0:T(8,128)(2,1)S(1)} %get-tuple-element.29), channel_id=1, source_target_pairs={{0,8},{2,10},{4,12},{6,14},{8,0},{10,2},{12,4},{14,6},{1,9},{3,11}... | collective-permute-start | bytes 221192 | tf_op jit(solution)/shard_map/ppermute | solution.py:353
  33.5 0.3 collective-permute-start.8
  33.8 4.2 %collective-permute-done.8.refs_3_ = f32[8,256]{1,0:T(8,128)S(1)} collective-permute-done((f32[8,256]{1,0:T(8,128)S(1)}, f32[8,256]{1,0:T(8,128)S(1)}, u32[]{:S(2)}, u32[]{:S(2)}) %collective-permute-start.8) | collective-permute-done | bytes 8224 | tf_op jit(solution)/shard_map/ppermute | solution.py:353
  38.0 0.0 collective-permute-done.7.refs_2_
  38.0 2.1 %back.1 = (f32[8,4096]{1,0:T(8,128)}, f32[8,32,128]{2,1,0:T(8,128)}) custom-call(s32[5]{0:T(128)S(1)} %stack.27.refs_0_, f32[8,4608]{1,0:T(8,128)S(1)} %get-tuple-element.28.refs_1_, s16[16,2304]{1,0:T(8,128)(2,1)S(1)} %collective-permute-done.7.refs_2_, f32[8,256]{1,0:T(8,128)S(1)} %collective-permute-done.8.refs_3_, ...), custom_call_target="tpu_custom_call" | custom-call | tf_op jit(solution)/shard_map/back/pallas_call | solution.py:482
  (6 shorter events, 0.0 us)
Async XLA Ops:
  1.6 2.3 %collective-permute-start = (bf16[2,256,128]{2,1,0:T(8,128)(2,1)S(1)}, bf16[2,256,128]{2,1,0:T(8,128)(2,1)S(1)}, u32[]{:S(2)}, u32[]{:S(2)}) collective-permute-start(bf16[2,256,128]{2,1,0:T(8,128)(2,1)S(1)} %constant_dynamic-slice_fusion), channel_id=1, source_target_pairs={{0,1},{1,0},{2,3},{3,2},{4,5},{5,4},{6,7},{7,6},{8,9},{9,8},{10,11... | collective-permute-start | bytes 393224 | tf_op jit(solution)/shard_map/ppermute | solution.py:353
  3.8 14.6 %copy-start.1 = (f32[32,128]{1,0:T(8,128)S(1)}, f32[32,128]{1,0:T(8,128)}, u32[]{:S(2)}) copy-start(f32[32,128]{1,0:T(8,128)} %param.13) | copy-start | bytes 49156
  3.9 14.6 %copy-start.2 = (s32[32,128]{1,0:T(8,128)S(1)}, s32[32,128]{1,0:T(8,128)}, u32[]{:S(2)}) copy-start(s32[32,128]{1,0:T(8,128)} %param.12) | copy-start | bytes 49156
  3.9 19.7 %copy-start.3 = (s32[3,8]{1,0:T(4,128)S(1)}, s32[3,8]{1,0:T(4,128)}, u32[]{:S(2)}) copy-start(s32[3,8]{1,0:T(4,128)} %param.11) | copy-start | bytes 292
  3.9 34.1 %copy-start = (bf16[512,512]{1,0:T(8,128)(2,1)S(1)}, bf16[512,512]{1,0:T(8,128)(2,1)}, u32[]{:S(2)}) copy-start(bf16[512,512]{1,0:T(8,128)(2,1)} %constant.26.clone.refs_6_) | copy-start | bytes 1572868
  15.3 8.2 %collective-permute-start.2 = (f32[8,256]{1,0:T(8,128)S(1)}, f32[8,256]{1,0:T(8,128)S(1)}, u32[]{:S(2)}, u32[]{:S(2)}) collective-permute-start(f32[8,256]{1,0:T(8,128)S(1)} %get-tuple-element.24), channel_id=1, source_target_pairs={{0,2},{2,0},{4,6},{6,4},{8,10},{10,8},{12,14},{14,12},{1,3},{3,1},... | collective-permute-start | bytes 24584 | tf_op jit(solution)/shard_map/ppermute | solution.py:353
  17.9 2.0 %collective-permute-start.3 = (f32[8,128]{1,0:T(8,128)S(1)}, f32[8,128]{1,0:T(8,128)S(1)}, u32[]{:S(2)}, u32[]{:S(2)}) collective-permute-start(f32[8,128]{1,0:T(8,128)S(1)} %slice.3), channel_id=1, source_target_pairs={{0,1},{1,0},{2,3},{3,2},{4,5},{5,4},{6,7},{7,6},{8,9},{9,8},{10,11... | collective-permute-start | bytes 12296 | tf_op jit(solution)/shard_map/ppermute | solution.py:353
  18.1 4.5 %collective-permute-start.1 = (s16[16,2304]{1,0:T(8,128)(2,1)S(1)}, s16[16,2304]{1,0:T(8,128)(2,1)S(1)}, u32[]{:S(2)}, u32[]{:S(2)}) collective-permute-start(s16[16,2304]{1,0:T(8,128)(2,1)S(1)} %get-tuple-element.20), channel_id=1, source_target_pairs={{0,2},{2,0},{4,6},{6,4},{8,10},{10,8},{12,14},{14,12},{1,3},{3,1},... | collective-permute-start | bytes 221192 | tf_op jit(solution)/shard_map/ppermute | solution.py:353
  19.9 3.7 %collective-permute-start.4 = (f32[8,128]{1,0:T(8,128)S(1)}, f32[8,128]{1,0:T(8,128)S(1)}, u32[]{:S(2)}, u32[]{:S(2)}) collective-permute-start(f32[8,128]{1,0:T(8,128)S(1)} %collective-permute-done.3.refs_4_), channel_id=1, source_target_pairs={{0,2},{2,0},{4,6},{6,4},{8,10},{10,8},{12,14},{14,12},{1,3},{3,1},... | collective-permute-start | bytes 12296 | tf_op jit(solution)/shard_map/ppermute | solution.py:353
  24.5 5.5 %collective-permute-start.5 = (s16[16,2304]{1,0:T(8,128)(2,1)S(1)}, s16[16,2304]{1,0:T(8,128)(2,1)S(1)}, u32[]{:S(2)}, u32[]{:S(2)}) collective-permute-start(s16[16,2304]{1,0:T(8,128)(2,1)S(1)} %get-tuple-element.26), channel_id=1, source_target_pairs={{0,4},{2,6},{4,0},{6,2},{8,12},{10,14},{12,8},{14,10},{1,5},{3,7},... | collective-permute-start | bytes 221192 | tf_op jit(solution)/shard_map/ppermute | solution.py:353
  26.3 3.7 %collective-permute-start.6 = (f32[8,256]{1,0:T(8,128)S(1)}, f32[8,256]{1,0:T(8,128)S(1)}, u32[]{:S(2)}, u32[]{:S(2)}) collective-permute-start(f32[8,256]{1,0:T(8,128)S(1)} %get-tuple-element.27), channel_id=1, source_target_pairs={{0,4},{2,6},{4,0},{6,2},{8,12},{10,14},{12,8},{14,10},{1,5},{3,7},... | collective-permute-start | bytes 24584 | tf_op jit(solution)/shard_map/ppermute | solution.py:353
  30.8 7.2 %collective-permute-start.7 = (s16[16,2304]{1,0:T(8,128)(2,1)S(1)}, s16[16,2304]{1,0:T(8,128)(2,1)S(1)}, u32[]{:S(2)}, u32[]{:S(2)}) collective-permute-start(s16[16,2304]{1,0:T(8,128)(2,1)S(1)} %get-tuple-element.29), channel_id=1, source_target_pairs={{0,8},{2,10},{4,12},{6,14},{8,0},{10,2},{12,4},{14,6},{1,9},{3,11}... | collective-permute-start | bytes 221192 | tf_op jit(solution)/shard_map/ppermute | solution.py:353
  33.5 4.5 %collective-permute-start.8 = (f32[8,256]{1,0:T(8,128)S(1)}, f32[8,256]{1,0:T(8,128)S(1)}, u32[]{:S(2)}, u32[]{:S(2)}) collective-permute-start(f32[8,256]{1,0:T(8,128)S(1)} %get-tuple-element.30), channel_id=1, source_target_pairs={{0,8},{2,10},{4,12},{6,14},{8,0},{10,2},{12,4},{14,6},{1,9},{3,11}... | collective-permute-start | bytes 24584 | tf_op jit(solution)/shard_map/ppermute | solution.py:353
where the time goes:
time: 40.4 us; the launch traced here: 40.1 us
  Pallas kernels  15.2 us (38%)
  starting transfers between devices  10.5 us (26%)
  waiting for transfers between devices  9.44 us (23%)
  other arithmetic  3.16 us (8%)
  local copies, waits for them, and re-layouts  1.1 us (3%)
  between operations  0.75 us (2%)
    pallas_call x1, Pallas kernels, on_device(): pl.pallas_call(front, out_shape=(series_shape,) + sent_shapes, in_specs=[...  11.4 us
    ppermute x9, starting transfers between devices, swapped(): lax.ppermute(x, axis, [(i, i ^ distance) for i in range(lax.axis_size(axi...  10.5 us
    ppermute x9, waiting for transfers between devices, swapped(): lax.ppermute(x, axis, [(i, i ^ distance) for i in range(lax.axis_size(axi...  9.44 us
    pallas_call x1, Pallas kernels, on_device(): pl.pallas_call(back, out_shape=(jax.ShapeDtypeStruct((trials, frames), F3...  2.09 us
    pallas_call x2, Pallas kernels, on_device(): pl.pallas_call(merge, out_shape=shapes, in_specs=[SMEM] + [VMEM] * 6, out...  1.69 us
    reduce_sum x1, other arithmetic, template_weights(): template = jnp.sum(jnp.where(hit, tap_weight[:, :, None], 0.0), axis=1)  1.39 us
    concatenate x1, other arithmetic, on_device(): jnp.concatenate([table, jnp.pad(pfb_taps, ((0, 0), (0, wide - channels)))...  0.99 us
    dynamic_slice x1, local copies, waits for them, and re-layouts, on_device(): sent = lax.dynamic_slice_in_dim(voltages, start, halo_rows, axis=1)  0.92 us
  transfers between devices with their start and end apart: 9, of which 4 were waited for; matrix products, arithmetic and copies ran while one was open for 8% of the time, Pallas kernels for 0%

commit v1 on v0

--- a/solution.py
+++ b/solution.py
@@ -396,7 +396,7 @@
     else:
         raise NotImplementedError("tm")
 
-    chunk_tiles, pieces = 5, 8
+    chunk_tiles, pieces = 12, 4
     table = jnp.asarray(dft_table(channels, group))
     extended = lead + frames + tail
     width = lead + extended
@@ -437,17 +437,21 @@
     )(info, voltages, halo, packed)
 
     shift_rows = jnp.broadcast_to(cross_shift[:, :, None], cross_shift.shape + (LANES,))
-    (tap_index, tap_weight), sent = lax.optimization_barrier(((tap_index, tap_weight), sent))
-    weights = template_weights(tap_index, tap_weight, tail // LANES + 1)
     short = [level for level in range(levels) if trials * 2**level <= LANES]
     fused = len(short) == levels > 1
-    other = swapped(sent[1][:, :lead], "tm", 1)
+    response = sent[1][:, :lead]
+    other = swapped(response, "tm", 1)
     for level in range(levels - 1 if fused else levels):
         if level in short:
+            if level == min(1, levels - 2):
+                (tap_index, tap_weight), sent = lax.optimization_barrier(((tap_index, tap_weight), sent))
+                weights = template_weights(tap_index, tap_weight, tail // LANES + 1)
             received = [swapped(x, "freq", 2**level) for x in sent]
+            if level == min(1, levels - 2):
+                received[0], weights = lax.optimization_barrier((received[0], weights))
             if level == 0:
-                across = swapped(other, "freq", 1)
-                received[0], weights = lax.optimization_barrier((received[0], weights))
+                pairs = [(i, i ^ tm_size ^ 1) for i in range(freq_size * tm_size)]
+                across = lax.ppermute(response, ("freq", "tm"), pairs)
             shapes = (series_shape,) + (sent_shapes if level + 1 in short else ())
 
             def merge(*refs, level=level):

time: 40.4 us -> 38.4 us (0.950)
  waiting for transfers between devices: 9.44 us -> 8.13 us
    ppermute x9 -> x8, waiting for transfers between devices: 9.44 us -> 7.16 us  [swapped(): lax.ppermute(x, axis, [(i, i ^ distance) for i in range(lax.axis_size(axi...]
    ppermute x9 -> x8, starting transfers between devices: 10.5 us -> 8.82 us  [swapped(): lax.ppermute(x, axis, [(i, i ^ distance) for i in range(lax.axis_size(axi...]
    ppermute x0 -> x1, starting transfers between devices: none -> 1.5 us  [on_device(): across = lax.ppermute(response, ('freq', 'tm'), pairs)]
    ppermute x0 -> x1, waiting for transfers between devices: none -> 0.97 us  [on_device(): across = lax.ppermute(response, ('freq', 'tm'), pairs)]
    pallas_call x1, Pallas kernels: 11.4 us -> 11 us  [on_device(): pl.pallas_call(front, out_shape=(series_shape,) + sent_shapes, in_specs=[...]
  transfers between devices with their start and end apart: 9 -> 9, of which waited for: 4 -> 4; matrix products, arithmetic and copies ran while one was open for 8% -> 9% of each run, Pallas kernels for 0% -> 0%
where the time goes in v1:
time: 38.4 us; the launch traced here: 38.2 us
  Pallas kernels  14.8 us (39%)
  starting transfers between devices  10.3 us (27%)
  waiting for transfers between devices  8.13 us (21%)
  other arithmetic  3.16 us (8%)
  local copies, waits for them, and re-layouts  1.1 us (3%)
  between operations  0.73 us (2%)
    pallas_call x1, Pallas kernels, on_device(): pl.pallas_call(front, out_shape=(series_shape,) + sent_shapes, in_specs=[...  11 us
    ppermute x8, starting transfers between devices, swapped(): lax.ppermute(x, axis, [(i, i ^ distance) for i in range(lax.axis_size(axi...  8.82 us
    ppermute x8, waiting for transfers between devices, swapped(): lax.ppermute(x, axis, [(i, i ^ distance) for i in range(lax.axis_size(axi...  7.16 us
    pallas_call x1, Pallas kernels, on_device(): pl.pallas_call(back, out_shape=(jax.ShapeDtypeStruct((trials, frames), F3...  2.09 us
    pallas_call x2, Pallas kernels, on_device(): pl.pallas_call(merge, out_shape=shapes, in_specs=[SMEM] + [VMEM] * 6, out...  1.69 us
    ppermute x1, starting transfers between devices, on_device(): across = lax.ppermute(response, ('freq', 'tm'), pairs)  1.5 us
    reduce_sum x1, other arithmetic, template_weights(): template = jnp.sum(jnp.where(hit, tap_weight[:, :, None], 0.0), axis=1)  1.39 us
    concatenate x1, other arithmetic, on_device(): jnp.concatenate([table, jnp.pad(pfb_taps, ((0, 0), (0, wide - channels)))...  0.99 us
  transfers between devices with their start and end apart: 9, of which 4 were waited for; matrix products, arithmetic and copies ran while one was open for 9% of the time, Pallas kernels for 0%

profile of v1, /device:TPU:0, one launch (start us, length us, event | category | flops | bytes accessed | tf_op | source)
XLA Modules:
  0.0 38.2 jit_solution(8333462975020126464)
XLA Ops:
  0.6 0.9 %constant_dynamic-slice_fusion = bf16[2,256,128]{2,1,0:T(8,128)(2,1)S(1)} fusion(bf16[2,4096,128]{2,1,0:T(8,128)(2,1)} %refs_1_.1, s32[]{:T(128)S(6)} %select_n.9), kind=kLoop, calls=%fused_computation.19 | loop fusion | bytes 262148 | tf_op jit(solution)/shard_map/dynamic_slice | solution.py:394
  1.6 0.5 %collective-permute-start = (bf16[2,256,128]{2,1,0:T(8,128)(2,1)S(1)}, bf16[2,256,128]{2,1,0:T(8,128)(2,1)S(1)}, u32[]{:S(2)}, u32[]{:S(2)}) collective-permute-start(bf16[2,256,128]{2,1,0:T(8,128)(2,1)S(1)} %constant_dynamic-slice_fusion), channel_id=1, source_target_pairs={{0,1},{1,0},{2,3},{3,2},{4,5},{5,4},{6,7},{7,6},{8,9},{9,8},{10,11... | collective-permute-start | bytes 393224 | tf_op jit(solution)/shard_map/ppermute | solution.py:353
  2.1 0.7 %convert_element_type.16 = f32[7,64]{1,0:T(8,128)S(1)} convert(s32[7,64]{1,0:T(8,128)} %param.10) | non-fusion elementwise | flops 448 | bytes 3584 | tf_op jit(solution)/shard_map/convert_element_type | solution.py:408
  2.8 0.1 stack.27.refs_0_
  2.9 1.0 %select_maximum_fusion.refs_3_ = f32[280,256]{1,0:T(8,128)S(1)} fusion(f32[7,64]{1,0:T(8,128)S(1)} %convert_element_type.16, f32[16,128]{1,0:T(8,128)} %param.9, f32[256,256]{1,0:T(8,128)} %constant.25.clone), kind=kLoop, calls=%fused_computation.8 | loop fusion | flops 573440 | bytes 558848 | tf_op jit(solution)/shard_map/concatenate | solution.py:407
  3.8 0.0 copy-start.3
  3.9 0.0 copy-start.1
  3.9 0.0 copy-start.2
  3.9 0.0 copy-start
  3.9 0.0 collective-permute-done.refs_2_
  3.9 11.0 %front.1 = (f32[8,4608]{1,0:T(8,128)S(1)}, s16[16,2304]{1,0:T(8,128)(2,1)S(1)}, f32[8,256]{1,0:T(8,128)S(1)}) custom-call(s32[5]{0:T(128)S(1)} %stack.27.refs_0_, bf16[2,4096,128]{2,1,0:T(8,128)(2,1)} %refs_1_.1, bf16[2,256,128]{2,1,0:T(8,128)(2,1)S(1)} %collective-permute-done.refs_2_, f32[280,256]{1,0:T(8,128)S(1)} %select_maximum_fusion.refs_3_), custom_call_target="tpu_custom_call" | custom-call | flops 20000000000 | bytes 4096 | tf_op jit(solution)/shard_map/front/pallas_call | solution.py:420
  14.9 2.6 %collective-permute-start.1 = (s16[16,2304]{1,0:T(8,128)(2,1)S(1)}, s16[16,2304]{1,0:T(8,128)(2,1)S(1)}, u32[]{:S(2)}, u32[]{:S(2)}) collective-permute-start(s16[16,2304]{1,0:T(8,128)(2,1)S(1)} %get-tuple-element.18), channel_id=1, source_target_pairs={{0,2},{2,0},{4,6},{6,4},{8,10},{10,8},{12,14},{14,12},{1,3},{3,1},... | collective-permute-start | bytes 221192 | tf_op jit(solution)/shard_map/ppermute | solution.py:353
  17.5 0.1 collective-permute-start.2
  17.5 1.5 %collective-permute-start.4 = (f32[8,128]{1,0:T(8,128)S(1)}, f32[8,128]{1,0:T(8,128)S(1)}, u32[]{:S(2)}, u32[]{:S(2)}) collective-permute-start(f32[8,128]{1,0:T(8,128)S(1)} %slice.3), channel_id=1, source_target_pairs={{0,3},{1,2},{2,1},{3,0},{4,7},{5,6},{6,5},{7,4},{8,11},{9,10},{10,... | collective-permute-start | bytes 12296 | tf_op jit(solution)/shard_map/ppermute | solution.py:454
  19.0 0.6 %collective-permute-start.3 = (f32[8,128]{1,0:T(8,128)S(1)}, f32[8,128]{1,0:T(8,128)S(1)}, u32[]{:S(2)}, u32[]{:S(2)}) collective-permute-start(f32[8,128]{1,0:T(8,128)S(1)} %slice.3), channel_id=1, source_target_pairs={{0,1},{1,0},{2,3},{3,2},{4,5},{5,4},{6,7},{7,6},{8,9},{9,8},{10,11... | collective-permute-start | bytes 12296 | tf_op jit(solution)/shard_map/ppermute | solution.py:353
  19.6 1.0 %collective-permute-done.4.refs_5_ = f32[8,128]{1,0:T(8,128)S(1)} collective-permute-done((f32[8,128]{1,0:T(8,128)S(1)}, f32[8,128]{1,0:T(8,128)S(1)}, u32[]{:S(2)}, u32[]{:S(2)}) %collective-permute-start.4) | collective-permute-done | bytes 4128 | tf_op jit(solution)/shard_map/ppermute | solution.py:454
  20.6 0.5 %collective-permute-done.2.refs_3_ = f32[8,256]{1,0:T(8,128)S(1)} collective-permute-done((f32[8,256]{1,0:T(8,128)S(1)}, f32[8,256]{1,0:T(8,128)S(1)}, u32[]{:S(2)}, u32[]{:S(2)}) %collective-permute-start.2) | collective-permute-done | bytes 8224 | tf_op jit(solution)/shard_map/ppermute | solution.py:353
  21.1 0.0 collective-permute-done.1.refs_2_
  21.1 0.1 broadcast_in_dim.10.refs_6_.refs_4_
  21.2 0.8 %merge.2 = (f32[8,4608]{1,0:T(8,128)S(1)}, s16[16,2304]{1,0:T(8,128)(2,1)S(1)}, f32[8,256]{1,0:T(8,128)S(1)}) custom-call(s32[5]{0:T(128)S(1)} %stack.27.refs_0_, f32[8,4608]{1,0:T(8,128)S(1)} %get-tuple-element.17.refs_1_, s16[16,2304]{1,0:T(8,128)(2,1)S(1)} %collective-permute-done.1.refs_2_, f32[8,256]{1,0:T(8,128)S(1)} %collective-permute-done.2.refs_3_, ...), custom_call_target="tpu_custom_call" | custom-call | tf_op jit(solution)/shard_map/merge/pallas_call | solution.py:460
  22.1 1.6 %collective-permute-start.6 = (f32[8,256]{1,0:T(8,128)S(1)}, f32[8,256]{1,0:T(8,128)S(1)}, u32[]{:S(2)}, u32[]{:S(2)}) collective-permute-start(f32[8,256]{1,0:T(8,128)S(1)} %get-tuple-element.27), channel_id=1, source_target_pairs={{0,4},{2,6},{4,0},{6,2},{8,12},{10,14},{12,8},{14,10},{1,5},{3,7},... | collective-permute-start | bytes 24584 | tf_op jit(solution)/shard_map/ppermute | solution.py:353
  23.7 0.4 %collective-permute-start.5 = (s16[16,2304]{1,0:T(8,128)(2,1)S(1)}, s16[16,2304]{1,0:T(8,128)(2,1)S(1)}, u32[]{:S(2)}, u32[]{:S(2)}) collective-permute-start(s16[16,2304]{1,0:T(8,128)(2,1)S(1)} %get-tuple-element.23), channel_id=1, source_target_pairs={{0,4},{2,6},{4,0},{6,2},{8,12},{10,14},{12,8},{14,10},{1,5},{3,7},... | collective-permute-start | bytes 221192 | tf_op jit(solution)/shard_map/ppermute | solution.py:353
  24.1 1.4 %select_reduce_fusion = f32[32,256]{1,0:T(8,128)S(1)} fusion(f32[32,128]{1,0:T(8,128)S(1)} %copy-done.1, s32[32,128]{1,0:T(8,128)S(1)} %copy-done.2), kind=kLoop, calls=%fused_computation | loop fusion | flops 3137536 | bytes 65536 | tf_op jit(solution)/shard_map/reduce_sum | solution.py:358
  25.5 0.1 select_maximum_fusion.2.refs_5_
  25.7 2.4 %collective-permute-done.5.refs_2_ = s16[16,2304]{1,0:T(8,128)(2,1)S(1)} collective-permute-done((s16[16,2304]{1,0:T(8,128)(2,1)S(1)}, s16[16,2304]{1,0:T(8,128)(2,1)S(1)}, u32[]{:S(2)}, u32[]{:S(2)}) %collective-permute-start.5) | collective-permute-done | bytes 73760 | tf_op jit(solution)/shard_map/ppermute | solution.py:353
  28.0 0.0 collective-permute-done.6.refs_3_
  28.1 0.8 %merge.3 = (f32[8,4608]{1,0:T(8,128)S(1)}, s16[16,2304]{1,0:T(8,128)(2,1)S(1)}, f32[8,256]{1,0:T(8,128)S(1)}) custom-call(s32[5]{0:T(128)S(1)} %stack.27.refs_0_, f32[8,4608]{1,0:T(8,128)S(1)} %get-tuple-element.20.refs_1_, s16[16,2304]{1,0:T(8,128)(2,1)S(1)} %collective-permute-done.5.refs_2_, f32[8,256]{1,0:T(8,128)S(1)} %collective-permute-done.6.refs_3_, ...), custom_call_target="tpu_custom_call" | custom-call | tf_op jit(solution)/shard_map/merge/pallas_call | solution.py:460
  28.9 2.7 %collective-permute-start.7 = (s16[16,2304]{1,0:T(8,128)(2,1)S(1)}, s16[16,2304]{1,0:T(8,128)(2,1)S(1)}, u32[]{:S(2)}, u32[]{:S(2)}) collective-permute-start(s16[16,2304]{1,0:T(8,128)(2,1)S(1)} %get-tuple-element.29), channel_id=1, source_target_pairs={{0,8},{2,10},{4,12},{6,14},{8,0},{10,2},{12,4},{14,6},{1,9},{3,11}... | collective-permute-start | bytes 221192 | tf_op jit(solution)/shard_map/ppermute | solution.py:353
  31.6 0.3 collective-permute-start.8
  31.9 4.2 %collective-permute-done.8.refs_3_ = f32[8,256]{1,0:T(8,128)S(1)} collective-permute-done((f32[8,256]{1,0:T(8,128)S(1)}, f32[8,256]{1,0:T(8,128)S(1)}, u32[]{:S(2)}, u32[]{:S(2)}) %collective-permute-start.8) | collective-permute-done | bytes 8224 | tf_op jit(solution)/shard_map/ppermute | solution.py:353
  36.1 0.0 collective-permute-done.7.refs_2_
  36.1 2.1 %back.1 = (f32[8,4096]{1,0:T(8,128)}, f32[8,32,128]{2,1,0:T(8,128)}) custom-call(s32[5]{0:T(128)S(1)} %stack.27.refs_0_, f32[8,4608]{1,0:T(8,128)S(1)} %get-tuple-element.28.refs_1_, s16[16,2304]{1,0:T(8,128)(2,1)S(1)} %collective-permute-done.7.refs_2_, f32[8,256]{1,0:T(8,128)S(1)} %collective-permute-done.8.refs_3_, ...), custom_call_target="tpu_custom_call" | custom-call | tf_op jit(solution)/shard_map/back/pallas_call | solution.py:486
  (6 shorter events, 0.0 us)
Async XLA Ops:
  1.6 2.3 %collective-permute-start = (bf16[2,256,128]{2,1,0:T(8,128)(2,1)S(1)}, bf16[2,256,128]{2,1,0:T(8,128)(2,1)S(1)}, u32[]{:S(2)}, u32[]{:S(2)}) collective-permute-start(bf16[2,256,128]{2,1,0:T(8,128)(2,1)S(1)} %constant_dynamic-slice_fusion), channel_id=1, source_target_pairs={{0,1},{1,0},{2,3},{3,2},{4,5},{5,4},{6,7},{7,6},{8,9},{9,8},{10,11... | collective-permute-start | bytes 393224 | tf_op jit(solution)/shard_map/ppermute | solution.py:353
  3.8 17.3 %copy-start.3 = (s32[3,8]{1,0:T(4,128)S(1)}, s32[3,8]{1,0:T(4,128)}, u32[]{:S(2)}) copy-start(s32[3,8]{1,0:T(4,128)} %param.11) | copy-start | bytes 292
  3.9 20.3 %copy-start.1 = (f32[32,128]{1,0:T(8,128)S(1)}, f32[32,128]{1,0:T(8,128)}, u32[]{:S(2)}) copy-start(f32[32,128]{1,0:T(8,128)} %param.13) | copy-start | bytes 49156
  3.9 20.3 %copy-start.2 = (s32[32,128]{1,0:T(8,128)S(1)}, s32[32,128]{1,0:T(8,128)}, u32[]{:S(2)}) copy-start(s32[32,128]{1,0:T(8,128)} %param.12) | copy-start | bytes 49156
  3.9 32.2 %copy-start = (bf16[512,512]{1,0:T(8,128)(2,1)S(1)}, bf16[512,512]{1,0:T(8,128)(2,1)}, u32[]{:S(2)}) copy-start(bf16[512,512]{1,0:T(8,128)(2,1)} %constant.26.clone.refs_6_) | copy-start | bytes 1572868
  14.9 6.2 %collective-permute-start.1 = (s16[16,2304]{1,0:T(8,128)(2,1)S(1)}, s16[16,2304]{1,0:T(8,128)(2,1)S(1)}, u32[]{:S(2)}, u32[]{:S(2)}) collective-permute-start(s16[16,2304]{1,0:T(8,128)(2,1)S(1)} %get-tuple-element.18), channel_id=1, source_target_pairs={{0,2},{2,0},{4,6},{6,4},{8,10},{10,8},{12,14},{14,12},{1,3},{3,1},... | collective-permute-start | bytes 221192 | tf_op jit(solution)/shard_map/ppermute | solution.py:353
  17.5 3.7 %collective-permute-start.2 = (f32[8,256]{1,0:T(8,128)S(1)}, f32[8,256]{1,0:T(8,128)S(1)}, u32[]{:S(2)}, u32[]{:S(2)}) collective-permute-start(f32[8,256]{1,0:T(8,128)S(1)} %get-tuple-element.19), channel_id=1, source_target_pairs={{0,2},{2,0},{4,6},{6,4},{8,10},{10,8},{12,14},{14,12},{1,3},{3,1},... | collective-permute-start | bytes 24584 | tf_op jit(solution)/shard_map/ppermute | solution.py:353
  17.5 3.0 %collective-permute-start.4 = (f32[8,128]{1,0:T(8,128)S(1)}, f32[8,128]{1,0:T(8,128)S(1)}, u32[]{:S(2)}, u32[]{:S(2)}) collective-permute-start(f32[8,128]{1,0:T(8,128)S(1)} %slice.3), channel_id=1, source_target_pairs={{0,3},{1,2},{2,1},{3,0},{4,7},{5,6},{6,5},{7,4},{8,11},{9,10},{10,... | collective-permute-start | bytes 12296 | tf_op jit(solution)/shard_map/ppermute | solution.py:454
  19.0 1.5 %collective-permute-start.3 = (f32[8,128]{1,0:T(8,128)S(1)}, f32[8,128]{1,0:T(8,128)S(1)}, u32[]{:S(2)}, u32[]{:S(2)}) collective-permute-start(f32[8,128]{1,0:T(8,128)S(1)} %slice.3), channel_id=1, source_target_pairs={{0,1},{1,0},{2,3},{3,2},{4,5},{5,4},{6,7},{7,6},{8,9},{9,8},{10,11... | collective-permute-start | bytes 12296 | tf_op jit(solution)/shard_map/ppermute | solution.py:353
  22.1 6.0 %collective-permute-start.6 = (f32[8,256]{1,0:T(8,128)S(1)}, f32[8,256]{1,0:T(8,128)S(1)}, u32[]{:S(2)}, u32[]{:S(2)}) collective-permute-start(f32[8,256]{1,0:T(8,128)S(1)} %get-tuple-element.27), channel_id=1, source_target_pairs={{0,4},{2,6},{4,0},{6,2},{8,12},{10,14},{12,8},{14,10},{1,5},{3,7},... | collective-permute-start | bytes 24584 | tf_op jit(solution)/shard_map/ppermute | solution.py:353
  23.7 4.4 %collective-permute-start.5 = (s16[16,2304]{1,0:T(8,128)(2,1)S(1)}, s16[16,2304]{1,0:T(8,128)(2,1)S(1)}, u32[]{:S(2)}, u32[]{:S(2)}) collective-permute-start(s16[16,2304]{1,0:T(8,128)(2,1)S(1)} %get-tuple-element.23), channel_id=1, source_target_pairs={{0,4},{2,6},{4,0},{6,2},{8,12},{10,14},{12,8},{14,10},{1,5},{3,7},... | collective-permute-start | bytes 221192 | tf_op jit(solution)/shard_map/ppermute | solution.py:353
  28.9 7.2 %collective-permute-start.7 = (s16[16,2304]{1,0:T(8,128)(2,1)S(1)}, s16[16,2304]{1,0:T(8,128)(2,1)S(1)}, u32[]{:S(2)}, u32[]{:S(2)}) collective-permute-start(s16[16,2304]{1,0:T(8,128)(2,1)S(1)} %get-tuple-element.29), channel_id=1, source_target_pairs={{0,8},{2,10},{4,12},{6,14},{8,0},{10,2},{12,4},{14,6},{1,9},{3,11}... | collective-permute-start | bytes 221192 | tf_op jit(solution)/shard_map/ppermute | solution.py:353
  31.6 4.5 %collective-permute-start.8 = (f32[8,256]{1,0:T(8,128)S(1)}, f32[8,256]{1,0:T(8,128)S(1)}, u32[]{:S(2)}, u32[]{:S(2)}) collective-permute-start(f32[8,256]{1,0:T(8,128)S(1)} %get-tuple-element.30), channel_id=1, source_target_pairs={{0,8},{2,10},{4,12},{6,14},{8,0},{10,2},{12,4},{14,6},{1,9},{3,11}... | collective-permute-start | bytes 24584 | tf_op jit(solution)/shard_map/ppermute | solution.py:353

commit v2 on v1

--- a/solution.py
+++ b/solution.py
@@ -69,7 +69,7 @@
     phase = (np.arange(channels)[:, None] * number[None, :]) % channels
     angle = phase * (2.0 * np.pi / channels)
     cosine, sine = np.cos(angle), np.sin(angle)
-    return np.block([[cosine, -sine], [sine, cosine]]).astype(np.float32)
+    return np.block([[cosine, -sine], [sine, cosine]]).T.astype(np.float32)
 
 
 def spread_table(tiles, blocks):
@@ -149,13 +149,13 @@
     def transform(slot, count):
         rows = slice(0, count * LANES)
         both = jnp.concatenate([filtered[slot][0][rows, :], filtered[slot][1][rows, :]], axis=1)
-        spectra[slot][rows, :] = jnp.dot(
-            both, packed[:taps_at, :], preferred_element_type=F32, precision=lax.Precision.HIGH
+        spectra[slot][:, rows] = lax.dot_general(
+            packed[:taps_at, :], both, NT, preferred_element_type=F32, precision=lax.Precision.HIGH
         )
 
     def collapse_tile(number, slot, sub, earlier):
-        real, imag = spectra[slot][tile(sub), :channels], spectra[slot][tile(sub), channels:]
-        power = (real * real + imag * imag).T
+        real, imag = spectra[slot][:channels, tile(sub)], spectra[slot][channels:, tile(sub)]
+        power = real * real + imag * imag
         counted = lead_tiles <= number < lead_tiles + main_tiles
         acc = jnp.zeros((ROWS, LANES), F32)
         now = []
@@ -335,13 +335,9 @@
         ],
         axis=0,
     )
-    one = grouped.astype(BF)
-    rest = grouped - one.astype(F32)
-    two = rest.astype(BF)
-    three = (rest - two.astype(F32)).astype(BF)
-    placed = jnp.dot(jnp.concatenate([one, two, three], axis=0), spread[...], preferred_element_type=F32)
+    placed = jnp.dot(jnp.concatenate(split(grouped), axis=0), spread[...], preferred_element_type=F32)
     count = sets * templates
-    placed = placed[:count] + placed[count : 2 * count] + placed[2 * count :]
+    placed = placed[:count] + placed[count:]
     trials = LANES // main_tiles
     positions = main_tiles * blocks
     for a in range(sets):
@@ -405,7 +401,7 @@
     wide = 2 * channels
     spare = ((0, -(tap_count + local_levels) % ROWS), (0, wide - local_shift.shape[1]))
     packed = jnp.concatenate(
-        [table, jnp.pad(pfb_taps, ((0, 0), (0, wide - channels))), jnp.pad(local_shift.astype(F32), spare)], axis=0
+        [table, jnp.pad(pfb_taps, ((0, 0), (0, wide - channels))), jnp.pad(local_shift, spare).astype(F32)], axis=0
     )
 
     def front(*refs):
@@ -426,7 +422,7 @@
             pltpu.VMEM(voltages.shape, BF),
             pltpu.VMEM((2, margin + extended, channels), F32),
             *[pltpu.VMEM((chunk_tiles * LANES, channels), F32)] * 4,
-            *[pltpu.VMEM((chunk_tiles * LANES, 2 * channels), F32)] * 2,
+            *[pltpu.VMEM((2 * channels, chunk_tiles * LANES), F32)] * 2,
             pltpu.VMEM((trials, width), F32),
             pltpu.VMEM((channels, LANES), F32),
             pltpu.SemaphoreType.DMA((pieces,)),
@@ -491,7 +487,7 @@
         ),
         in_specs=[SMEM] + [VMEM] * 6,
         out_specs=(VMEM, VMEM),
-        scratch_shapes=[pltpu.VMEM(((frames + tail) // LANES * ROWS, LANES), F32)],
+        scratch_shapes=[pltpu.VMEM(((frames + tail) // LANES * ROWS + ROWS, LANES), F32)],
         compiler_params=PARAMS,
         name="back",
     )(info, series, *received, shift_rows, weights, spread)

time: 38.4 us -> 37.3 us (0.971)
  Pallas kernels: 14.8 us -> 13.6 us
    pallas_call x1, Pallas kernels: 11 us -> 9.89 us  [on_device(): pl.pallas_call(front, out_shape=(series_shape,) + sent_shapes, in_specs=[...]
where the time goes in v2:
time: 37.3 us; the launch traced here: 37 us
  Pallas kernels  13.6 us (36%)
  starting transfers between devices  10.3 us (28%)
  waiting for transfers between devices  8.13 us (22%)
  other arithmetic  3.16 us (8%)
  local copies, waits for them, and re-layouts  1.1 us (3%)
  between operations  0.73 us (2%)
    pallas_call x1, Pallas kernels, on_device(): pl.pallas_call(front, out_shape=(series_shape,) + sent_shapes, in_specs=[...  9.89 us
    ppermute x8, starting transfers between devices, swapped(): lax.ppermute(x, axis, [(i, i ^ distance) for i in range(lax.axis_size(axi...  8.81 us
    ppermute x8, waiting for transfers between devices, swapped(): lax.ppermute(x, axis, [(i, i ^ distance) for i in range(lax.axis_size(axi...  7.16 us
    pallas_call x1, Pallas kernels, on_device(): pl.pallas_call(back, out_shape=(jax.ShapeDtypeStruct((trials, frames), F3...  2.02 us
    pallas_call x2, Pallas kernels, on_device(): pl.pallas_call(merge, out_shape=shapes, in_specs=[SMEM] + [VMEM] * 6, out...  1.69 us
    ppermute x1, starting transfers between devices, on_device(): across = lax.ppermute(response, ('freq', 'tm'), pairs)  1.5 us
    reduce_sum x1, other arithmetic, template_weights(): template = jnp.sum(jnp.where(hit, tap_weight[:, :, None], 0.0), axis=1)  1.39 us
    concatenate x1, other arithmetic, on_device(): jnp.concatenate([table, jnp.pad(pfb_taps, ((0, 0), (0, wide - channels)))...  0.99 us
  transfers between devices with their start and end apart: 9, of which 4 were waited for; matrix products, arithmetic and copies ran while one was open for 9% of the time, Pallas kernels for 0%

profile of v2, /device:TPU:0, one launch (start us, length us, event | category | flops | bytes accessed | tf_op | source)
XLA Modules:
  0.0 37.0 jit_solution(9775757067385842882)
XLA Ops:
  0.6 0.9 %constant_dynamic-slice_fusion = bf16[2,256,128]{2,1,0:T(8,128)(2,1)S(1)} fusion(bf16[2,4096,128]{2,1,0:T(8,128)(2,1)} %refs_1_.1, s32[]{:T(128)S(6)} %select_n.9), kind=kLoop, calls=%fused_computation.19 | loop fusion | bytes 262148 | tf_op jit(solution)/shard_map/dynamic_slice | solution.py:390
  1.6 0.5 %collective-permute-start = (bf16[2,256,128]{2,1,0:T(8,128)(2,1)S(1)}, bf16[2,256,128]{2,1,0:T(8,128)(2,1)S(1)}, u32[]{:S(2)}, u32[]{:S(2)}) collective-permute-start(bf16[2,256,128]{2,1,0:T(8,128)(2,1)S(1)} %constant_dynamic-slice_fusion), channel_id=1, source_target_pairs={{0,1},{1,0},{2,3},{3,2},{4,5},{5,4},{6,7},{7,6},{8,9},{9,8},{10,11... | collective-permute-start | bytes 393224 | tf_op jit(solution)/shard_map/ppermute | solution.py:349
  2.1 0.7 %pad_convert_fusion = f32[8,256]{1,0:T(8,128)S(1)} fusion(s32[7,64]{1,0:T(8,128)} %param.10), kind=kLoop, calls=%fused_computation.18 | loop fusion | flops 2048 | bytes 9984 | tf_op jit(solution)/shard_map/convert_element_type | solution.py:404
  2.8 0.1 stack.27.refs_0_
  2.9 1.0 %fusion.refs_3_ = f32[280,256]{1,0:T(8,128)S(1)} fusion(f32[16,128]{1,0:T(8,128)} %param.9, f32[8,256]{1,0:T(8,128)S(1)} %pad_convert_fusion, f32[256,256]{1,0:T(8,128)} %constant.25.clone), kind=kLoop, calls=%fused_computation.9 | loop fusion | flops 430080 | bytes 565248 | tf_op jit(solution)/shard_map/concatenate | solution.py:403
  3.8 0.0 copy-start.3
  3.9 0.0 copy-start.1
  3.9 0.0 copy-start.2
  3.9 0.0 copy-start
  3.9 0.0 collective-permute-done.refs_2_
  3.9 9.9 %front.1 = (f32[8,4608]{1,0:T(8,128)S(1)}, s16[16,2304]{1,0:T(8,128)(2,1)S(1)}, f32[8,256]{1,0:T(8,128)S(1)}) custom-call(s32[5]{0:T(128)S(1)} %stack.27.refs_0_, bf16[2,4096,128]{2,1,0:T(8,128)(2,1)} %refs_1_.1, bf16[2,256,128]{2,1,0:T(8,128)(2,1)S(1)} %collective-permute-done.refs_2_, f32[280,256]{1,0:T(8,128)S(1)} %fusion.refs_3_), custom_call_target="tpu_custom_call" | custom-call | flops 20000000000 | bytes 4096 | tf_op jit(solution)/shard_map/front/pallas_call | solution.py:416
  13.8 2.6 %collective-permute-start.1 = (s16[16,2304]{1,0:T(8,128)(2,1)S(1)}, s16[16,2304]{1,0:T(8,128)(2,1)S(1)}, u32[]{:S(2)}, u32[]{:S(2)}) collective-permute-start(s16[16,2304]{1,0:T(8,128)(2,1)S(1)} %get-tuple-element.18), channel_id=1, source_target_pairs={{0,2},{2,0},{4,6},{6,4},{8,10},{10,8},{12,14},{14,12},{1,3},{3,1},... | collective-permute-start | bytes 221192 | tf_op jit(solution)/shard_map/ppermute | solution.py:349
  16.4 0.1 collective-permute-start.2
  16.4 1.5 %collective-permute-start.4 = (f32[8,128]{1,0:T(8,128)S(1)}, f32[8,128]{1,0:T(8,128)S(1)}, u32[]{:S(2)}, u32[]{:S(2)}) collective-permute-start(f32[8,128]{1,0:T(8,128)S(1)} %slice.3), channel_id=1, source_target_pairs={{0,3},{1,2},{2,1},{3,0},{4,7},{5,6},{6,5},{7,4},{8,11},{9,10},{10,... | collective-permute-start | bytes 12296 | tf_op jit(solution)/shard_map/ppermute | solution.py:450
  18.0 0.6 %collective-permute-start.3 = (f32[8,128]{1,0:T(8,128)S(1)}, f32[8,128]{1,0:T(8,128)S(1)}, u32[]{:S(2)}, u32[]{:S(2)}) collective-permute-start(f32[8,128]{1,0:T(8,128)S(1)} %slice.3), channel_id=1, source_target_pairs={{0,1},{1,0},{2,3},{3,2},{4,5},{5,4},{6,7},{7,6},{8,9},{9,8},{10,11... | collective-permute-start | bytes 12296 | tf_op jit(solution)/shard_map/ppermute | solution.py:349
  18.5 1.0 %collective-permute-done.4.refs_5_ = f32[8,128]{1,0:T(8,128)S(1)} collective-permute-done((f32[8,128]{1,0:T(8,128)S(1)}, f32[8,128]{1,0:T(8,128)S(1)}, u32[]{:S(2)}, u32[]{:S(2)}) %collective-permute-start.4) | collective-permute-done | bytes 4128 | tf_op jit(solution)/shard_map/ppermute | solution.py:450
  19.5 0.0 collective-permute-done.3.refs_4_
  19.5 0.5 %collective-permute-done.2.refs_3_ = f32[8,256]{1,0:T(8,128)S(1)} collective-permute-done((f32[8,256]{1,0:T(8,128)S(1)}, f32[8,256]{1,0:T(8,128)S(1)}, u32[]{:S(2)}, u32[]{:S(2)}) %collective-permute-start.2) | collective-permute-done | bytes 8224 | tf_op jit(solution)/shard_map/ppermute | solution.py:349
  20.0 0.0 collective-permute-done.1.refs_2_
  20.0 0.1 broadcast_in_dim.10.refs_6_.refs_4_
  20.1 0.8 %merge.2 = (f32[8,4608]{1,0:T(8,128)S(1)}, s16[16,2304]{1,0:T(8,128)(2,1)S(1)}, f32[8,256]{1,0:T(8,128)S(1)}) custom-call(s32[5]{0:T(128)S(1)} %stack.27.refs_0_, f32[8,4608]{1,0:T(8,128)S(1)} %get-tuple-element.17.refs_1_, s16[16,2304]{1,0:T(8,128)(2,1)S(1)} %collective-permute-done.1.refs_2_, f32[8,256]{1,0:T(8,128)S(1)} %collective-permute-done.2.refs_3_, ...), custom_call_target="tpu_custom_call" | custom-call | tf_op jit(solution)/shard_map/merge/pallas_call | solution.py:456
  21.0 1.6 %collective-permute-start.6 = (f32[8,256]{1,0:T(8,128)S(1)}, f32[8,256]{1,0:T(8,128)S(1)}, u32[]{:S(2)}, u32[]{:S(2)}) collective-permute-start(f32[8,256]{1,0:T(8,128)S(1)} %get-tuple-element.27), channel_id=1, source_target_pairs={{0,4},{2,6},{4,0},{6,2},{8,12},{10,14},{12,8},{14,10},{1,5},{3,7},... | collective-permute-start | bytes 24584 | tf_op jit(solution)/shard_map/ppermute | solution.py:349
  22.6 0.4 %collective-permute-start.5 = (s16[16,2304]{1,0:T(8,128)(2,1)S(1)}, s16[16,2304]{1,0:T(8,128)(2,1)S(1)}, u32[]{:S(2)}, u32[]{:S(2)}) collective-permute-start(s16[16,2304]{1,0:T(8,128)(2,1)S(1)} %get-tuple-element.23), channel_id=1, source_target_pairs={{0,4},{2,6},{4,0},{6,2},{8,12},{10,14},{12,8},{14,10},{1,5},{3,7},... | collective-permute-start | bytes 221192 | tf_op jit(solution)/shard_map/ppermute | solution.py:349
  23.0 1.4 %select_reduce_fusion = f32[32,256]{1,0:T(8,128)S(1)} fusion(f32[32,128]{1,0:T(8,128)S(1)} %copy-done.1, s32[32,128]{1,0:T(8,128)S(1)} %copy-done.2), kind=kLoop, calls=%fused_computation | loop fusion | flops 3137536 | bytes 65536 | tf_op jit(solution)/shard_map/reduce_sum | solution.py:354
  24.4 0.1 select_maximum_fusion.1.refs_5_
  24.6 2.4 %collective-permute-done.5.refs_2_ = s16[16,2304]{1,0:T(8,128)(2,1)S(1)} collective-permute-done((s16[16,2304]{1,0:T(8,128)(2,1)S(1)}, s16[16,2304]{1,0:T(8,128)(2,1)S(1)}, u32[]{:S(2)}, u32[]{:S(2)}) %collective-permute-start.5) | collective-permute-done | bytes 73760 | tf_op jit(solution)/shard_map/ppermute | solution.py:349
  26.9 0.0 collective-permute-done.6.refs_3_
  27.0 0.8 %merge.3 = (f32[8,4608]{1,0:T(8,128)S(1)}, s16[16,2304]{1,0:T(8,128)(2,1)S(1)}, f32[8,256]{1,0:T(8,128)S(1)}) custom-call(s32[5]{0:T(128)S(1)} %stack.27.refs_0_, f32[8,4608]{1,0:T(8,128)S(1)} %get-tuple-element.20.refs_1_, s16[16,2304]{1,0:T(8,128)(2,1)S(1)} %collective-permute-done.5.refs_2_, f32[8,256]{1,0:T(8,128)S(1)} %collective-permute-done.6.refs_3_, ...), custom_call_target="tpu_custom_call" | custom-call | tf_op jit(solution)/shard_map/merge/pallas_call | solution.py:456
  27.8 2.7 %collective-permute-start.7 = (s16[16,2304]{1,0:T(8,128)(2,1)S(1)}, s16[16,2304]{1,0:T(8,128)(2,1)S(1)}, u32[]{:S(2)}, u32[]{:S(2)}) collective-permute-start(s16[16,2304]{1,0:T(8,128)(2,1)S(1)} %get-tuple-element.29), channel_id=1, source_target_pairs={{0,8},{2,10},{4,12},{6,14},{8,0},{10,2},{12,4},{14,6},{1,9},{3,11}... | collective-permute-start | bytes 221192 | tf_op jit(solution)/shard_map/ppermute | solution.py:349
  30.5 0.3 collective-permute-start.8
  30.8 4.2 %collective-permute-done.8.refs_3_ = f32[8,256]{1,0:T(8,128)S(1)} collective-permute-done((f32[8,256]{1,0:T(8,128)S(1)}, f32[8,256]{1,0:T(8,128)S(1)}, u32[]{:S(2)}, u32[]{:S(2)}) %collective-permute-start.8) | collective-permute-done | bytes 8224 | tf_op jit(solution)/shard_map/ppermute | solution.py:349
  35.0 2.0 %back.1 = (f32[8,4096]{1,0:T(8,128)}, f32[8,32,128]{2,1,0:T(8,128)}) custom-call(s32[5]{0:T(128)S(1)} %stack.27.refs_0_, f32[8,4608]{1,0:T(8,128)S(1)} %get-tuple-element.28.refs_1_, s16[16,2304]{1,0:T(8,128)(2,1)S(1)} %collective-permute-done.7.refs_2_, f32[8,256]{1,0:T(8,128)S(1)} %collective-permute-done.8.refs_3_, ...), custom_call_target="tpu_custom_call" | custom-call | tf_op jit(solution)/shard_map/back/pallas_call | solution.py:482
  (6 shorter events, 0.0 us)
Async XLA Ops:
  1.6 2.3 %collective-permute-start = (bf16[2,256,128]{2,1,0:T(8,128)(2,1)S(1)}, bf16[2,256,128]{2,1,0:T(8,128)(2,1)S(1)}, u32[]{:S(2)}, u32[]{:S(2)}) collective-permute-start(bf16[2,256,128]{2,1,0:T(8,128)(2,1)S(1)} %constant_dynamic-slice_fusion), channel_id=1, source_target_pairs={{0,1},{1,0},{2,3},{3,2},{4,5},{5,4},{6,7},{7,6},{8,9},{9,8},{10,11... | collective-permute-start | bytes 393224 | tf_op jit(solution)/shard_map/ppermute | solution.py:349
  3.8 16.2 %copy-start.3 = (s32[3,8]{1,0:T(4,128)S(1)}, s32[3,8]{1,0:T(4,128)}, u32[]{:S(2)}) copy-start(s32[3,8]{1,0:T(4,128)} %param.11) | copy-start | bytes 292
  3.9 19.2 %copy-start.1 = (f32[32,128]{1,0:T(8,128)S(1)}, f32[32,128]{1,0:T(8,128)}, u32[]{:S(2)}) copy-start(f32[32,128]{1,0:T(8,128)} %param.13) | copy-start | bytes 49156
  3.9 19.2 %copy-start.2 = (s32[32,128]{1,0:T(8,128)S(1)}, s32[32,128]{1,0:T(8,128)}, u32[]{:S(2)}) copy-start(s32[32,128]{1,0:T(8,128)} %param.12) | copy-start | bytes 49156
  3.9 31.1 %copy-start = (bf16[512,512]{1,0:T(8,128)(2,1)S(1)}, bf16[512,512]{1,0:T(8,128)(2,1)}, u32[]{:S(2)}) copy-start(bf16[512,512]{1,0:T(8,128)(2,1)} %constant.26.clone.refs_6_) | copy-start | bytes 1572868
  13.8 6.2 %collective-permute-start.1 = (s16[16,2304]{1,0:T(8,128)(2,1)S(1)}, s16[16,2304]{1,0:T(8,128)(2,1)S(1)}, u32[]{:S(2)}, u32[]{:S(2)}) collective-permute-start(s16[16,2304]{1,0:T(8,128)(2,1)S(1)} %get-tuple-element.18), channel_id=1, source_target_pairs={{0,2},{2,0},{4,6},{6,4},{8,10},{10,8},{12,14},{14,12},{1,3},{3,1},... | collective-permute-start | bytes 221192 | tf_op jit(solution)/shard_map/ppermute | solution.py:349
  16.4 3.7 %collective-permute-start.2 = (f32[8,256]{1,0:T(8,128)S(1)}, f32[8,256]{1,0:T(8,128)S(1)}, u32[]{:S(2)}, u32[]{:S(2)}) collective-permute-start(f32[8,256]{1,0:T(8,128)S(1)} %get-tuple-element.19), channel_id=1, source_target_pairs={{0,2},{2,0},{4,6},{6,4},{8,10},{10,8},{12,14},{14,12},{1,3},{3,1},... | collective-permute-start | bytes 24584 | tf_op jit(solution)/shard_map/ppermute | solution.py:349
  16.4 3.0 %collective-permute-start.4 = (f32[8,128]{1,0:T(8,128)S(1)}, f32[8,128]{1,0:T(8,128)S(1)}, u32[]{:S(2)}, u32[]{:S(2)}) collective-permute-start(f32[8,128]{1,0:T(8,128)S(1)} %slice.3), channel_id=1, source_target_pairs={{0,3},{1,2},{2,1},{3,0},{4,7},{5,6},{6,5},{7,4},{8,11},{9,10},{10,... | collective-permute-start | bytes 12296 | tf_op jit(solution)/shard_map/ppermute | solution.py:450
  18.0 1.5 %collective-permute-start.3 = (f32[8,128]{1,0:T(8,128)S(1)}, f32[8,128]{1,0:T(8,128)S(1)}, u32[]{:S(2)}, u32[]{:S(2)}) collective-permute-start(f32[8,128]{1,0:T(8,128)S(1)} %slice.3), channel_id=1, source_target_pairs={{0,1},{1,0},{2,3},{3,2},{4,5},{5,4},{6,7},{7,6},{8,9},{9,8},{10,11... | collective-permute-start | bytes 12296 | tf_op jit(solution)/shard_map/ppermute | solution.py:349
  21.0 6.0 %collective-permute-start.6 = (f32[8,256]{1,0:T(8,128)S(1)}, f32[8,256]{1,0:T(8,128)S(1)}, u32[]{:S(2)}, u32[]{:S(2)}) collective-permute-start(f32[8,256]{1,0:T(8,128)S(1)} %get-tuple-element.27), channel_id=1, source_target_pairs={{0,4},{2,6},{4,0},{6,2},{8,12},{10,14},{12,8},{14,10},{1,5},{3,7},... | collective-permute-start | bytes 24584 | tf_op jit(solution)/shard_map/ppermute | solution.py:349
  22.6 4.4 %collective-permute-start.5 = (s16[16,2304]{1,0:T(8,128)(2,1)S(1)}, s16[16,2304]{1,0:T(8,128)(2,1)S(1)}, u32[]{:S(2)}, u32[]{:S(2)}) collective-permute-start(s16[16,2304]{1,0:T(8,128)(2,1)S(1)} %get-tuple-element.23), channel_id=1, source_target_pairs={{0,4},{2,6},{4,0},{6,2},{8,12},{10,14},{12,8},{14,10},{1,5},{3,7},... | collective-permute-start | bytes 221192 | tf_op jit(solution)/shard_map/ppermute | solution.py:349
  27.8 7.2 %collective-permute-start.7 = (s16[16,2304]{1,0:T(8,128)(2,1)S(1)}, s16[16,2304]{1,0:T(8,128)(2,1)S(1)}, u32[]{:S(2)}, u32[]{:S(2)}) collective-permute-start(s16[16,2304]{1,0:T(8,128)(2,1)S(1)} %get-tuple-element.29), channel_id=1, source_target_pairs={{0,8},{2,10},{4,12},{6,14},{8,0},{10,2},{12,4},{14,6},{1,9},{3,11}... | collective-permute-start | bytes 221192 | tf_op jit(solution)/shard_map/ppermute | solution.py:349
  30.5 4.5 %collective-permute-start.8 = (f32[8,256]{1,0:T(8,128)S(1)}, f32[8,256]{1,0:T(8,128)S(1)}, u32[]{:S(2)}, u32[]{:S(2)}) collective-permute-start(f32[8,256]{1,0:T(8,128)S(1)} %get-tuple-element.30), channel_id=1, source_target_pairs={{0,8},{2,10},{4,12},{6,14},{8,0},{10,2},{12,4},{14,6},{1,9},{3,11}... | collective-permute-start | bytes 24584 | tf_op jit(solution)/shard_map/ppermute | solution.py:349

commit v3 on v2

--- a/solution.py
+++ b/solution.py
@@ -83,13 +83,13 @@
 
 
 def front_kernel(
-    sizes, info, volts, beside, packed, out, words, notes, held, samples, *scratch
+    sizes, info, volts, beside, packed, shifts, out, words, notes, held, samples, *scratch
 ):
     filtered, spectra = (scratch[:2], scratch[2:4]), scratch[4:6]
     series, sums, arrived = scratch[6:]
     frames, lead, tail, chunk_tiles, pieces, tap_count, level_count, columns = sizes
     channels = volts.shape[2]
-    taps_at, shifts_at = 2 * channels, 2 * channels + tap_count
+    taps_at = 2 * channels
     group_count = channels // ROWS
     margin = round_up(tap_count, 16)
     halo_rows = beside.shape[1]
@@ -110,7 +110,7 @@
     single_levels = group_count.bit_length() - 1
 
     def picked(hit, level):
-        row = jnp.broadcast_to(packed[shifts_at + level : shifts_at + level + 1, :columns], (LANES, columns))
+        row = jnp.broadcast_to(shifts[level : level + 1, :].astype(F32), (LANES, columns))
         return lax.dot_general(hit.astype(F32), row, NT, preferred_element_type=F32)
 
     total = jnp.zeros((channels, LANES), F32)
@@ -392,17 +392,14 @@
     else:
         raise NotImplementedError("tm")
 
-    chunk_tiles, pieces = 12, 4
+    chunk_tiles, pieces = 18, 4
     table = jnp.asarray(dft_table(channels, group))
     extended = lead + frames + tail
     width = lead + extended
 
     sizes = (frames, lead, tail, chunk_tiles, pieces, tap_count) + local_shift.shape
     wide = 2 * channels
-    spare = ((0, -(tap_count + local_levels) % ROWS), (0, wide - local_shift.shape[1]))
-    packed = jnp.concatenate(
-        [table, jnp.pad(pfb_taps, ((0, 0), (0, wide - channels))), jnp.pad(local_shift, spare).astype(F32)], axis=0
-    )
+    packed = jnp.concatenate([table, jnp.pad(pfb_taps, ((0, 0), (0, wide - channels)))], axis=0)
 
     def front(*refs):
         front_kernel(sizes, *refs)
@@ -416,7 +413,7 @@
     series, *sent = pl.pallas_call(
         front,
         out_shape=(series_shape,) + sent_shapes,
-        in_specs=[SMEM, ANY, VMEM, VMEM],
+        in_specs=[SMEM, ANY, VMEM, VMEM, VMEM],
         out_specs=(VMEM,) * 3,
         scratch_shapes=[
             pltpu.VMEM(voltages.shape, BF),
@@ -430,7 +427,7 @@
         compiler_params=pltpu.CompilerParams(vmem_limit_bytes=52 * 1024 * 1024),
         cost_estimate=pl.CostEstimate(flops=2 * 10**10, bytes_accessed=4096, transcendentals=0),
         name="front",
-    )(info, voltages, halo, packed)
+    )(info, voltages, halo, packed, local_shift)
 
     shift_rows = jnp.broadcast_to(cross_shift[:, :, None], cross_shift.shape + (LANES,))
     short = [level for level in range(levels) if trials * 2**level <= LANES]

time: 37.3 us -> 37.4 us (level)
  local copies, waits for them, and re-layouts: 1.1 us -> 1.83 us
  other arithmetic: 3.16 us -> 2.47 us
    unnamed x8 -> x10, local copies, waits for them, and re-layouts: 0.03 us -> 0.75 us
    convert_element_type x1 -> x0, other arithmetic: 0.69 us -> none  [on_device(): jnp.pad(local_shift, spare).astype(F32)]
    ppermute x8, starting transfers between devices: 8.81 us -> 9.21 us  [swapped(): lax.ppermute(x, axis, [(i, i ^ distance) for i in range(lax.axis_size(axi...]
  transfers between devices with their start and end apart: 9 -> 9, of which waited for: 4 -> 4; matrix products, arithmetic and copies ran while one was open for 9% -> 7% of each run, Pallas kernels for 0% -> 0%
where the time goes in v3:
time: 37.4 us; the launch traced here: 37.1 us
  Pallas kernels  13.5 us (36%)
  starting transfers between devices  10.5 us (28%)
  waiting for transfers between devices  8.1 us (22%)
  other arithmetic  2.47 us (7%)
  local copies, waits for them, and re-layouts  1.83 us (5%)
  between operations  0.72 us (2%)
    pallas_call x1, Pallas kernels, on_device(): pl.pallas_call(front, out_shape=(series_shape,) + sent_shapes, in_specs=[...  9.77 us
    ppermute x8, starting transfers between devices, swapped(): lax.ppermute(x, axis, [(i, i ^ distance) for i in range(lax.axis_size(axi...  9.21 us
    ppermute x8, waiting for transfers between devices, swapped(): lax.ppermute(x, axis, [(i, i ^ distance) for i in range(lax.axis_size(axi...  7.16 us
    pallas_call x1, Pallas kernels, on_device(): pl.pallas_call(back, out_shape=(jax.ShapeDtypeStruct((trials, frames), F3...  2.03 us
    pallas_call x2, Pallas kernels, on_device(): pl.pallas_call(merge, out_shape=shapes, in_specs=[SMEM] + [VMEM] * 6, out...  1.69 us
    reduce_sum x1, other arithmetic, template_weights(): template = jnp.sum(jnp.where(hit, tap_weight[:, :, None], 0.0), axis=1)  1.39 us
    ppermute x1, starting transfers between devices, on_device(): across = lax.ppermute(response, ('freq', 'tm'), pairs)  1.31 us
    concatenate x1, other arithmetic, on_device(): jnp.concatenate([table, jnp.pad(pfb_taps, ((0, 0), (0, wide - channels)))...  0.99 us
  transfers between devices with their start and end apart: 9, of which 4 were waited for; matrix products, arithmetic and copies ran while one was open for 7% of the time, Pallas kernels for 0%

profile of v3, /device:TPU:0, one launch (start us, length us, event | category | flops | bytes accessed | tf_op | source)
XLA Modules:
  0.0 37.1 jit_solution(3390712268484635700)
XLA Ops:
  0.6 0.9 %constant_dynamic-slice_fusion = bf16[2,256,128]{2,1,0:T(8,128)(2,1)S(1)} fusion(bf16[2,4096,128]{2,1,0:T(8,128)(2,1)} %refs_1_.1, s32[]{:T(128)S(6)} %select_n.9), kind=kLoop, calls=%fused_computation.15 | loop fusion | bytes 262148 | tf_op jit(solution)/shard_map/dynamic_slice | solution.py:390
  1.6 0.5 %collective-permute-start = (bf16[2,256,128]{2,1,0:T(8,128)(2,1)S(1)}, bf16[2,256,128]{2,1,0:T(8,128)(2,1)S(1)}, u32[]{:S(2)}, u32[]{:S(2)}) collective-permute-start(bf16[2,256,128]{2,1,0:T(8,128)(2,1)S(1)} %constant_dynamic-slice_fusion), channel_id=1, source_target_pairs={{0,1},{1,0},{2,3},{3,2},{4,5},{5,4},{6,7},{7,6},{8,9},{9,8},{10,11... | collective-permute-start | bytes 393224 | tf_op jit(solution)/shard_map/ppermute | solution.py:349
  2.1 0.1 stack.27.refs_0_
  2.2 1.0 %select_maximum_fusion.refs_3_ = f32[272,256]{1,0:T(8,128)S(1)} fusion(f32[16,128]{1,0:T(8,128)} %param.9, f32[256,256]{1,0:T(8,128)} %constant.25.clone), kind=kLoop, calls=%fused_computation.6 | loop fusion | flops 208896 | bytes 548864 | tf_op jit(solution)/shard_map/concatenate | solution.py:402
  3.2 0.0 copy-start
  3.2 0.0 collective-permute-done.refs_2_
  3.2 0.0 copy-start.1
  3.2 0.7 %copy-done.1 = s32[7,64]{1,0:T(8,128)S(1)} copy-done((s32[7,64]{1,0:T(8,128)S(1)}, s32[7,64]{1,0:T(8,128)}, u32[]{:S(2)}) %copy-start.1) | copy-done | bytes 1816
  3.9 9.8 %front.1 = (f32[8,4608]{1,0:T(8,128)S(1)}, s16[16,2304]{1,0:T(8,128)(2,1)S(1)}, f32[8,256]{1,0:T(8,128)S(1)}) custom-call(s32[5]{0:T(128)S(1)} %stack.27.refs_0_, bf16[2,4096,128]{2,1,0:T(8,128)(2,1)} %refs_1_.1, bf16[2,256,128]{2,1,0:T(8,128)(2,1)S(1)} %collective-permute-done.refs_2_, f32[272,256]{1,0:T(8,128)S(1)} %select_maximum_fusion.refs_3_, ...), custom_call_target="tpu_custom_call" | custom-call | flops 20000000000 | bytes 4096 | tf_op jit(solution)/shard_map/front/pallas_call | solution.py:413
  13.7 2.8 %collective-permute-start.1 = (s16[16,2304]{1,0:T(8,128)(2,1)S(1)}, s16[16,2304]{1,0:T(8,128)(2,1)S(1)}, u32[]{:S(2)}, u32[]{:S(2)}) collective-permute-start(s16[16,2304]{1,0:T(8,128)(2,1)S(1)} %get-tuple-element.18), channel_id=1, source_target_pairs={{0,2},{2,0},{4,6},{6,4},{8,10},{10,8},{12,14},{14,12},{1,3},{3,1},... | collective-permute-start | bytes 221192 | tf_op jit(solution)/shard_map/ppermute | solution.py:349
  16.5 0.0 collective-permute-start.2
  16.5 1.3 %collective-permute-start.4 = (f32[8,128]{1,0:T(8,128)S(1)}, f32[8,128]{1,0:T(8,128)S(1)}, u32[]{:S(2)}, u32[]{:S(2)}) collective-permute-start(f32[8,128]{1,0:T(8,128)S(1)} %slice.3), channel_id=1, source_target_pairs={{0,3},{1,2},{2,1},{3,0},{4,7},{5,6},{6,5},{7,4},{8,11},{9,10},{10,... | collective-permute-start | bytes 12296 | tf_op jit(solution)/shard_map/ppermute | solution.py:447
  17.8 0.8 %collective-permute-start.3 = (f32[8,128]{1,0:T(8,128)S(1)}, f32[8,128]{1,0:T(8,128)S(1)}, u32[]{:S(2)}, u32[]{:S(2)}) collective-permute-start(f32[8,128]{1,0:T(8,128)S(1)} %slice.3), channel_id=1, source_target_pairs={{0,1},{1,0},{2,3},{3,2},{4,5},{5,4},{6,7},{7,6},{8,9},{9,8},{10,11... | collective-permute-start | bytes 12296 | tf_op jit(solution)/shard_map/ppermute | solution.py:349
  18.6 0.9 %collective-permute-done.4.refs_5_ = f32[8,128]{1,0:T(8,128)S(1)} collective-permute-done((f32[8,128]{1,0:T(8,128)S(1)}, f32[8,128]{1,0:T(8,128)S(1)}, u32[]{:S(2)}, u32[]{:S(2)}) %collective-permute-start.4) | collective-permute-done | bytes 4128 | tf_op jit(solution)/shard_map/ppermute | solution.py:447
  19.6 0.0 collective-permute-done.3.refs_4_
  19.6 0.6 %collective-permute-done.2.refs_3_ = f32[8,256]{1,0:T(8,128)S(1)} collective-permute-done((f32[8,256]{1,0:T(8,128)S(1)}, f32[8,256]{1,0:T(8,128)S(1)}, u32[]{:S(2)}, u32[]{:S(2)}) %collective-permute-start.2) | collective-permute-done | bytes 8224 | tf_op jit(solution)/shard_map/ppermute | solution.py:349
  20.1 0.0 collective-permute-done.1.refs_2_
  20.1 0.0 copy-done.4
  20.1 0.1 broadcast_in_dim.10.refs_6_.refs_4_
  20.2 0.8 %merge.2 = (f32[8,4608]{1,0:T(8,128)S(1)}, s16[16,2304]{1,0:T(8,128)(2,1)S(1)}, f32[8,256]{1,0:T(8,128)S(1)}) custom-call(s32[5]{0:T(128)S(1)} %stack.27.refs_0_, f32[8,4608]{1,0:T(8,128)S(1)} %get-tuple-element.17.refs_1_, s16[16,2304]{1,0:T(8,128)(2,1)S(1)} %collective-permute-done.1.refs_2_, f32[8,256]{1,0:T(8,128)S(1)} %collective-permute-done.2.refs_3_, ...), custom_call_target="tpu_custom_call" | custom-call | tf_op jit(solution)/shard_map/merge/pallas_call | solution.py:453
  21.1 1.6 %collective-permute-start.6 = (f32[8,256]{1,0:T(8,128)S(1)}, f32[8,256]{1,0:T(8,128)S(1)}, u32[]{:S(2)}, u32[]{:S(2)}) collective-permute-start(f32[8,256]{1,0:T(8,128)S(1)} %get-tuple-element.27), channel_id=1, source_target_pairs={{0,4},{2,6},{4,0},{6,2},{8,12},{10,14},{12,8},{14,10},{1,5},{3,7},... | collective-permute-start | bytes 24584 | tf_op jit(solution)/shard_map/ppermute | solution.py:349
  22.7 0.5 %collective-permute-start.5 = (s16[16,2304]{1,0:T(8,128)(2,1)S(1)}, s16[16,2304]{1,0:T(8,128)(2,1)S(1)}, u32[]{:S(2)}, u32[]{:S(2)}) collective-permute-start(s16[16,2304]{1,0:T(8,128)(2,1)S(1)} %get-tuple-element.23), channel_id=1, source_target_pairs={{0,4},{2,6},{4,0},{6,2},{8,12},{10,14},{12,8},{14,10},{1,5},{3,7},... | collective-permute-start | bytes 221192 | tf_op jit(solution)/shard_map/ppermute | solution.py:349
  23.2 1.4 %select_reduce_fusion = f32[32,256]{1,0:T(8,128)S(1)} fusion(f32[32,128]{1,0:T(8,128)S(1)} %copy-done.2, s32[32,128]{1,0:T(8,128)S(1)} %copy-done.3), kind=kLoop, calls=%fused_computation | loop fusion | flops 3137536 | bytes 65536 | tf_op jit(solution)/shard_map/reduce_sum | solution.py:354
  24.6 0.1 select_maximum_fusion.1.refs_5_
  24.7 2.4 %collective-permute-done.5.refs_2_ = s16[16,2304]{1,0:T(8,128)(2,1)S(1)} collective-permute-done((s16[16,2304]{1,0:T(8,128)(2,1)S(1)}, s16[16,2304]{1,0:T(8,128)(2,1)S(1)}, u32[]{:S(2)}, u32[]{:S(2)}) %collective-permute-start.5) | collective-permute-done | bytes 73760 | tf_op jit(solution)/shard_map/ppermute | solution.py:349
  27.0 0.0 collective-permute-done.6.refs_3_
  27.0 0.8 %merge.3 = (f32[8,4608]{1,0:T(8,128)S(1)}, s16[16,2304]{1,0:T(8,128)(2,1)S(1)}, f32[8,256]{1,0:T(8,128)S(1)}) custom-call(s32[5]{0:T(128)S(1)} %stack.27.refs_0_, f32[8,4608]{1,0:T(8,128)S(1)} %get-tuple-element.20.refs_1_, s16[16,2304]{1,0:T(8,128)(2,1)S(1)} %collective-permute-done.5.refs_2_, f32[8,256]{1,0:T(8,128)S(1)} %collective-permute-done.6.refs_3_, ...), custom_call_target="tpu_custom_call" | custom-call | tf_op jit(solution)/shard_map/merge/pallas_call | solution.py:453
  27.9 2.7 %collective-permute-start.7 = (s16[16,2304]{1,0:T(8,128)(2,1)S(1)}, s16[16,2304]{1,0:T(8,128)(2,1)S(1)}, u32[]{:S(2)}, u32[]{:S(2)}) collective-permute-start(s16[16,2304]{1,0:T(8,128)(2,1)S(1)} %get-tuple-element.29), channel_id=1, source_target_pairs={{0,8},{2,10},{4,12},{6,14},{8,0},{10,2},{12,4},{14,6},{1,9},{3,11}... | collective-permute-start | bytes 221192 | tf_op jit(solution)/shard_map/ppermute | solution.py:349
  30.6 0.3 collective-permute-start.8
  30.9 4.2 %collective-permute-done.8.refs_3_ = f32[8,256]{1,0:T(8,128)S(1)} collective-permute-done((f32[8,256]{1,0:T(8,128)S(1)}, f32[8,256]{1,0:T(8,128)S(1)}, u32[]{:S(2)}, u32[]{:S(2)}) %collective-permute-start.8) | collective-permute-done | bytes 8224 | tf_op jit(solution)/shard_map/ppermute | solution.py:349
  35.1 0.0 collective-permute-done.7.refs_2_
  35.1 2.0 %back.1 = (f32[8,4096]{1,0:T(8,128)}, f32[8,32,128]{2,1,0:T(8,128)}) custom-call(s32[5]{0:T(128)S(1)} %stack.27.refs_0_, f32[8,4608]{1,0:T(8,128)S(1)} %get-tuple-element.28.refs_1_, s16[16,2304]{1,0:T(8,128)(2,1)S(1)} %collective-permute-done.7.refs_2_, f32[8,256]{1,0:T(8,128)S(1)} %collective-permute-done.8.refs_3_, ...), custom_call_target="tpu_custom_call" | custom-call | tf_op jit(solution)/shard_map/back/pallas_call | solution.py:479
  (7 shorter events, 0.0 us)
Async XLA Ops:
  1.6 1.6 %collective-permute-start = (bf16[2,256,128]{2,1,0:T(8,128)(2,1)S(1)}, bf16[2,256,128]{2,1,0:T(8,128)(2,1)S(1)}, u32[]{:S(2)}, u32[]{:S(2)}) collective-permute-start(bf16[2,256,128]{2,1,0:T(8,128)(2,1)S(1)} %constant_dynamic-slice_fusion), channel_id=1, source_target_pairs={{0,1},{1,0},{2,3},{3,2},{4,5},{5,4},{6,7},{7,6},{8,9},{9,8},{10,11... | collective-permute-start | bytes 393224 | tf_op jit(solution)/shard_map/ppermute | solution.py:349
  3.2 32.0 %copy-start = (bf16[512,512]{1,0:T(8,128)(2,1)S(1)}, bf16[512,512]{1,0:T(8,128)(2,1)}, u32[]{:S(2)}) copy-start(bf16[512,512]{1,0:T(8,128)(2,1)} %constant.26.clone.refs_6_) | copy-start | bytes 1572868
  3.2 0.7 %copy-start.1 = (s32[7,64]{1,0:T(8,128)S(1)}, s32[7,64]{1,0:T(8,128)}, u32[]{:S(2)}) copy-start(s32[7,64]{1,0:T(8,128)} %refs_4_.1) | copy-start | bytes 5380
  3.9 16.2 %copy-start.4 = (s32[3,8]{1,0:T(4,128)S(1)}, s32[3,8]{1,0:T(4,128)}, u32[]{:S(2)}) copy-start(s32[3,8]{1,0:T(4,128)} %param.11) | copy-start | bytes 292
  3.9 19.2 %copy-start.2 = (f32[32,128]{1,0:T(8,128)S(1)}, f32[32,128]{1,0:T(8,128)}, u32[]{:S(2)}) copy-start(f32[32,128]{1,0:T(8,128)} %param.13) | copy-start | bytes 49156
  3.9 19.2 %copy-start.3 = (s32[32,128]{1,0:T(8,128)S(1)}, s32[32,128]{1,0:T(8,128)}, u32[]{:S(2)}) copy-start(s32[32,128]{1,0:T(8,128)} %param.12) | copy-start | bytes 49156
  13.7 6.4 %collective-permute-start.1 = (s16[16,2304]{1,0:T(8,128)(2,1)S(1)}, s16[16,2304]{1,0:T(8,128)(2,1)S(1)}, u32[]{:S(2)}, u32[]{:S(2)}) collective-permute-start(s16[16,2304]{1,0:T(8,128)(2,1)S(1)} %get-tuple-element.18), channel_id=1, source_target_pairs={{0,2},{2,0},{4,6},{6,4},{8,10},{10,8},{12,14},{14,12},{1,3},{3,1},... | collective-permute-start | bytes 221192 | tf_op jit(solution)/shard_map/ppermute | solution.py:349
  16.5 3.7 %collective-permute-start.2 = (f32[8,256]{1,0:T(8,128)S(1)}, f32[8,256]{1,0:T(8,128)S(1)}, u32[]{:S(2)}, u32[]{:S(2)}) collective-permute-start(f32[8,256]{1,0:T(8,128)S(1)} %get-tuple-element.19), channel_id=1, source_target_pairs={{0,2},{2,0},{4,6},{6,4},{8,10},{10,8},{12,14},{14,12},{1,3},{3,1},... | collective-permute-start | bytes 24584 | tf_op jit(solution)/shard_map/ppermute | solution.py:349
  16.5 3.0 %collective-permute-start.4 = (f32[8,128]{1,0:T(8,128)S(1)}, f32[8,128]{1,0:T(8,128)S(1)}, u32[]{:S(2)}, u32[]{:S(2)}) collective-permute-start(f32[8,128]{1,0:T(8,128)S(1)} %slice.3), channel_id=1, source_target_pairs={{0,3},{1,2},{2,1},{3,0},{4,7},{5,6},{6,5},{7,4},{8,11},{9,10},{10,... | collective-permute-start | bytes 12296 | tf_op jit(solution)/shard_map/ppermute | solution.py:447
  17.8 1.7 %collective-permute-start.3 = (f32[8,128]{1,0:T(8,128)S(1)}, f32[8,128]{1,0:T(8,128)S(1)}, u32[]{:S(2)}, u32[]{:S(2)}) collective-permute-start(f32[8,128]{1,0:T(8,128)S(1)} %slice.3), channel_id=1, source_target_pairs={{0,1},{1,0},{2,3},{3,2},{4,5},{5,4},{6,7},{7,6},{8,9},{9,8},{10,11... | collective-permute-start | bytes 12296 | tf_op jit(solution)/shard_map/ppermute | solution.py:349
  21.1 6.0 %collective-permute-start.6 = (f32[8,256]{1,0:T(8,128)S(1)}, f32[8,256]{1,0:T(8,128)S(1)}, u32[]{:S(2)}, u32[]{:S(2)}) collective-permute-start(f32[8,256]{1,0:T(8,128)S(1)} %get-tuple-element.27), channel_id=1, source_target_pairs={{0,4},{2,6},{4,0},{6,2},{8,12},{10,14},{12,8},{14,10},{1,5},{3,7},... | collective-permute-start | bytes 24584 | tf_op jit(solution)/shard_map/ppermute | solution.py:349
  22.7 4.4 %collective-permute-start.5 = (s16[16,2304]{1,0:T(8,128)(2,1)S(1)}, s16[16,2304]{1,0:T(8,128)(2,1)S(1)}, u32[]{:S(2)}, u32[]{:S(2)}) collective-permute-start(s16[16,2304]{1,0:T(8,128)(2,1)S(1)} %get-tuple-element.23), channel_id=1, source_target_pairs={{0,4},{2,6},{4,0},{6,2},{8,12},{10,14},{12,8},{14,10},{1,5},{3,7},... | collective-permute-start | bytes 221192 | tf_op jit(solution)/shard_map/ppermute | solution.py:349
  27.9 7.2 %collective-permute-start.7 = (s16[16,2304]{1,0:T(8,128)(2,1)S(1)}, s16[16,2304]{1,0:T(8,128)(2,1)S(1)}, u32[]{:S(2)}, u32[]{:S(2)}) collective-permute-start(s16[16,2304]{1,0:T(8,128)(2,1)S(1)} %get-tuple-element.29), channel_id=1, source_target_pairs={{0,8},{2,10},{4,12},{6,14},{8,0},{10,2},{12,4},{14,6},{1,9},{3,11}... | collective-permute-start | bytes 221192 | tf_op jit(solution)/shard_map/ppermute | solution.py:349
  30.6 4.5 %collective-permute-start.8 = (f32[8,256]{1,0:T(8,128)S(1)}, f32[8,256]{1,0:T(8,128)S(1)}, u32[]{:S(2)}, u32[]{:S(2)}) collective-permute-start(f32[8,256]{1,0:T(8,128)S(1)} %get-tuple-element.30), channel_id=1, source_target_pairs={{0,8},{2,10},{4,12},{6,14},{8,0},{10,2},{12,4},{14,6},{1,9},{3,11}... | collective-permute-start | bytes 24584 | tf_op jit(solution)/shard_map/ppermute | solution.py:349
